TPU v7x, 256 devices: a whole 4x4x8 slice. The times are simulated.
256 devices in a mesh: segment: 4 (over y), rows: 64 (over z, x, core).
Axes of the slice: x: 4, y: 4, z: 8, core: 2. Of those that a mesh axis runs over, the one named last changes fastest.
Arguments:
- state: bfloat16 [4, 2, 128, 23040], P('segment', None, 'rows'), may hold values from -6 to 6
- bounds: int32 [5], replicated, may hold values from 0 to 5, as said below
- timesteps: int32 [2], replicated, may hold values from 0 to 999
- gains: float32 [4, 2, 320], P('segment'), may hold values from 0.1 to 1.9
- spatial_weight: bfloat16 [4, 2, 3, 3, 320, 320], P('segment'), may hold values from -0.109375 to 0.109375
- temporal_weight: bfloat16 [4, 2, 3, 320, 320], P('segment'), may hold values from -0.1875 to 0.1875
- time_weight: float32 [4, 2, 320, 320], P('segment'), may hold values from -0.5 to 0.5
Outputs:
- new_state: bfloat16 [4, 2, 128, 23040], P('segment', None, 'rows')
Inputs may be any that keep to these rules, and one draw needn't show every extreme that they name: bounds[0] = 0, bounds[4] = 5, and every component holds 1 or 2 blocks; slot 1 of a component with one block may be computed but is not kept.
All inputs are finite; a program needn't handle non-finite values.
Results may differ from a plain program's by a relative error of at most 0.0065.
Values may be sent and summed in bfloat16 or wider, within the bound.
A program may use at most 64 MiB of HBM per device.

v0:
```python
import math

import jax
import jax.numpy as jnp
from jax import lax
from jax.sharding import PartitionSpec as P

C = 320
W = 72
STEPS = 2


def from_behind(value, axis, by):
    length = lax.axis_size(axis)
    return lax.ppermute(value, axis, [(i, (i + by) % length) for i in range(length)])


def with_halo(value, sides, width):
    for axis, dim in sides:
        size, length = (lax.axis_size(axis), value.shape[dim])
        up = [(i, (i + 1) % size) for i in range(size - 1)]
        down = [(j, i) for i, j in up]
        last = lax.slice_in_dim(value, length - width, length, axis=dim)
        initial = lax.slice_in_dim(value, 0, width, axis=dim)
        before = lax.ppermute(last, axis, up)
        after = lax.ppermute(initial, axis, down)
        value = jnp.concatenate([before, value, after], axis=dim)
    return value


def embed(step_time, entries):
    half = entries // 2
    freq = jnp.exp(-math.log(10000.0) * jnp.arange(half, dtype=jnp.float32) / half)
    angle = step_time.astype(jnp.float32) * freq
    return jnp.concatenate([jnp.cos(angle), jnp.sin(angle)])


def block_rows(extended, gain, spatial, temporal, bias):
    values = extended.astype(jnp.float32)
    scale = lax.rsqrt(jnp.mean(values * values, axis=-1, keepdims=True) + 1e-06)
    normed = (values * scale * gain).astype(jnp.bfloat16)
    padded = jnp.pad(normed, ((0, 0), (0, 0), (1, 1), (0, 0)))
    frames, rows_in, width, chans = extended.shape
    rows_out = rows_in - 2
    total = jnp.zeros((frames * rows_out * width, chans), jnp.float32) + bias
    for shift_y in range(3):
        for shift_x in range(3):
            window = padded[:, shift_y : shift_y + rows_out, shift_x : shift_x + width, :].reshape(
                -1, chans
            )
            total = total + jnp.dot(
                window, spatial[shift_y, shift_x], preferred_element_type=jnp.float32
            )
    activated = jax.nn.silu(total).astype(jnp.bfloat16).reshape(frames, rows_out, width, chans)
    framed = jnp.pad(activated, ((1, 1), (0, 0), (0, 0), (0, 0)))
    mixed = jnp.zeros_like(total)
    for tap in range(3):
        mixed = mixed + jnp.dot(
            framed[tap : tap + frames].reshape(-1, chans),
            temporal[tap],
            preferred_element_type=jnp.float32,
        )
    center = extended[:, 1:-1].astype(jnp.float32).reshape(-1, chans)
    return (center + total + mixed).astype(jnp.bfloat16).reshape(frames, rows_out, width, chans)


def clear_outside(extended, row_group, rows_dev, groups):
    margin = (extended.shape[1] - rows_dev) // 2
    global_row = row_group * rows_dev - margin + jnp.arange(extended.shape[1], dtype=jnp.int32)
    inside = (global_row >= 0) & (global_row < rows_dev * groups)
    return jnp.where(inside[None, :, None, None], extended, jnp.zeros_like(extended))


def body(state, bounds, timesteps, gains, spatial_weight, temporal_weight, time_weight):
    frames = state.shape[1]
    rows_dev = state.shape[2]
    groups = lax.axis_size("rows")
    segment_pos = lax.axis_index("segment")
    row_group = lax.axis_index("rows")
    count = bounds[segment_pos + 1] - bounds[segment_pos]
    fields = state.reshape(frames, rows_dev, W, C)
    for step in range(STEPS):
        emb = embed(timesteps[step], time_weight.shape[2])
        bias_all = jnp.einsum("t,jtc->jc", emb, time_weight[0], precision=lax.Precision.HIGHEST)
        current = from_behind(fields, "segment", 1)

        def apply(slot, extended):
            return block_rows(
                extended,
                gains[0, slot],
                spatial_weight[0, slot],
                temporal_weight[0, slot],
                bias_all[slot],
            )

        def with_rim(slot, field):
            extended = with_halo(field, (("rows", 1),), 1)
            return apply(slot, clear_outside(extended, row_group, rows_dev, groups))

        current = with_rim(0, current)
        second = with_rim(1, current)
        current = jnp.where(count > 1, second, current)
        fields = current
    return fields.reshape(1, frames, rows_dev, W * C)


def solution(mesh):
    placed = (
        P("segment", None, "rows", None),
        P(),
        P(),
        P("segment", None, None),
        P("segment", None, None, None, None, None),
        P("segment", None, None, None, None),
        P("segment", None, None, None),
    )
    return jax.shard_map(
        body,
        mesh=mesh,
        in_specs=placed,
        out_specs=P("segment", None, "rows", None),
        check_vma=False,
    )
```

profile of v0, /device:TPU:103, one launch (start us, length us, event | category | flops | bytes accessed | tf_op | source)
XLA Modules:
  0.0 92.0 jit_solution(10249169461006113667)
XLA Ops:
  0.0 1.9 %reshape.267 = bf16[2,2,72,320]{3,2,1,0:T(8,128)(2,1)} reshape(bf16[1,2,2,23040]{3,2,1,0:T(2,128)(2,1)} %param.7) | data formatting | bytes 368640 | tf_op jit(solution)/shard_map/reshape | solution.py:81
  1.9 1.3 %collective-permute-start = (bf16[2,2,72,320]{3,2,1,0:T(8,128)(2,1)}, bf16[2,2,72,320]{3,2,1,0:T(8,128)(2,1)S(1)}, u32[]{:S(2)}, u32[]{:S(2)}) collective-permute-start(bf16[2,2,72,320]{3,2,1,0:T(8,128)(2,1)} %reshape.267), channel_id=1, source_target_pairs={{0,64},{64,128},{128,192},{192,0},{1,65},{65,129},{129,193},{193,1... | collective-permute-start | bytes 552968 | tf_op jit(solution)/shard_map/ppermute | solution.py:15
  3.2 1.3 %fusion.63 = (s32[1]{0:T(128)}, s32[1]{0:T(128)}) fusion(s32[2]{0:T(128)} %param.9), kind=kLoop, calls=%fused_computation.196 | loop fusion | bytes 16 | tf_op jit(solution)/shard_map/slice | solution.py:83
  6.0 0.6 fusion.11
  6.6 4.1 %slice_bitcast_fusion = (bf16[3,3,320,320]{3,2,1,0:T(8,128)(2,1)S(1)}, bf16[3,3,320,320]{3,2,1,0:T(8,128)(2,1)}) fusion(bf16[1,2,3,3,320,320]{5,4,3,2,1,0:T(8,128)(2,1)} %param.11), kind=kLoop, calls=%fused_computation | loop fusion | bytes 7372800 | tf_op jit(solution)/shard_map/squeeze | solution.py:91
  10.8 5.5 %collective-permute-start.1 = (bf16[2,1,72,320]{3,2,1,0:T(8,128)(2,1)S(1)}, bf16[2,1,72,320]{3,2,1,0:T(8,128)(2,1)S(1)}, u32[]{:S(2)}, u32[]{:S(2)}) collective-permute-start(bf16[2,1,72,320]{3,2,1,0:T(8,128)(2,1)S(1)} %get-tuple-element.71), channel_id=1, source_target_pairs={{0,1},{1,2},{2,3},{3,4},{4,5},{5,6},{6,7},{7,8},{8,9},{9,10},{10,1... | collective-permute-start | bytes 276488 | tf_op jit(solution)/shard_map/ppermute | solution.py:25
  16.3 1.9 %collective-permute-start.2 = (bf16[2,1,72,320]{3,2,1,0:T(8,128)(2,1)S(1)}, bf16[2,1,72,320]{3,2,1,0:T(8,128)(2,1)S(1)}, u32[]{:S(2)}, u32[]{:S(2)}) collective-permute-start(bf16[2,1,72,320]{3,2,1,0:T(8,128)(2,1)S(1)} %get-tuple-element.72), channel_id=1, source_target_pairs={{1,0},{2,1},{3,2},{4,3},{5,4},{6,5},{7,6},{8,7},{9,8},{10,9},{11,1... | collective-permute-start | bytes 276488 | tf_op jit(solution)/shard_map/ppermute | solution.py:26
  18.3 7.4 %collective-permute-done.2 = bf16[2,1,72,320]{3,2,1,0:T(8,128)(2,1)S(1)} collective-permute-done((bf16[2,1,72,320]{3,2,1,0:T(8,128)(2,1)S(1)}, bf16[2,1,72,320]{3,2,1,0:T(8,128)(2,1)S(1)}, u32[]{:S(2)}, u32[]{:S(2)}) %collective-permute-start.2) | collective-permute-done | bytes 92192 | tf_op jit(solution)/shard_map/ppermute | solution.py:26
  26.5 1.1 %copy-done.1 = bf16[3,3,320,320]{3,2,1,0:T(8,128)(2,1)S(1)} copy-done((bf16[3,3,320,320]{3,2,1,0:T(8,128)(2,1)S(1)}, bf16[3,3,320,320]{3,2,1,0:T(8,128)(2,1)}, u32[]{:S(2)}) %copy-start.1) | copy-done | bytes 1843224
  29.6 0.3 convolution_add_fusion.37
  30.2 0.4 multiply_convert_fusion.3
  30.6 0.6 copy-done.3
  31.6 0.3 convolution_add_fusion.34
  31.9 0.3 fusion.4
  32.2 0.7 fusion.61
  32.9 1.9 %collective-permute-start.3 = (bf16[2,1,72,320]{3,2,1,0:T(8,128)(2,1)}, bf16[2,1,72,320]{3,2,1,0:T(8,128)(2,1)}, u32[]{:S(2)}, u32[]{:S(2)}) collective-permute-start(bf16[2,1,72,320]{3,2,1,0:T(8,128)(2,1)} %get-tuple-element.67), channel_id=1, source_target_pairs={{0,1},{1,2},{2,3},{3,4},{4,5},{5,6},{6,7},{7,8},{8,9},{9,10},{10,1... | collective-permute-start | bytes 276488 | tf_op jit(solution)/shard_map/ppermute | solution.py:25
  34.8 2.4 %collective-permute-start.4 = (bf16[2,1,72,320]{3,2,1,0:T(8,128)(2,1)S(1)}, bf16[2,1,72,320]{3,2,1,0:T(8,128)(2,1)}, u32[]{:S(2)}, u32[]{:S(2)}) collective-permute-start(bf16[2,1,72,320]{3,2,1,0:T(8,128)(2,1)S(1)} %get-tuple-element.68), channel_id=1, source_target_pairs={{1,0},{2,1},{3,2},{4,3},{5,4},{6,5},{7,6},{8,7},{9,8},{10,9},{11,1... | collective-permute-start | bytes 276488 | tf_op jit(solution)/shard_map/ppermute | solution.py:26
  37.3 0.7 fusion.64
  39.3 5.0 %collective-permute-done.4 = bf16[2,1,72,320]{3,2,1,0:T(8,128)(2,1)} collective-permute-done((bf16[2,1,72,320]{3,2,1,0:T(8,128)(2,1)S(1)}, bf16[2,1,72,320]{3,2,1,0:T(8,128)(2,1)}, u32[]{:S(2)}, u32[]{:S(2)}) %collective-permute-start.4) | collective-permute-done | bytes 92192 | tf_op jit(solution)/shard_map/ppermute | solution.py:26
  44.3 1.3 %fusion.16 = (f32[2,4,72]{2,1,0:T(4,128)S(1)}, bf16[2,4,72,320]{3,2,1,0:T(8,128)(2,1)S(1)}) fusion(bf16[2,1,72,320]{3,2,1,0:T(8,128)(2,1)} %collective-permute-done.4, bf16[2,2,72,320]{3,2,1,0:T(8,128)(2,1)S(1)} %bitcast.240, bf16[2,1,72,320]{3,2,1,0:T(8,128)(2,1)} %collective-permute-done.3, pred[4]{0:T(512)(128)(4,1)S(1)} %compare_and_fusion), kind=kLoop, calls=%fused_computation.70 | loop fusion | flops 1105344 | bytes 739588 | tf_op jit(solution)/shard_map/reduce_sum | solution.py:40
  46.1 0.3 convolution_add_fusion.32
  47.0 0.3 convolution_add_fusion.29
  47.7 0.3 convolution_add_fusion.27
  48.6 0.4 multiply_convert_fusion.2
  49.1 0.6 copy-done.4
  50.3 0.3 fusion.5
  50.7 1.4 %collective-permute-start.5 = (bf16[2,2,72,320]{3,2,1,0:T(8,128)(2,1)S(1)}, bf16[2,2,72,320]{3,2,1,0:T(8,128)(2,1)S(1)}, u32[]{:S(2)}, u32[]{:S(2)}) collective-permute-start(bf16[2,2,72,320]{3,2,1,0:T(8,128)(2,1)S(1)} %broadcast_select_fusion), channel_id=1, source_target_pairs={{0,64},{64,128},{128,192},{192,0},{1,65},{65,129},{129,193},{193,1... | collective-permute-start | bytes 552968 | tf_op jit(solution)/shard_map/ppermute | solution.py:15
  52.1 0.5 fusion.9
  52.6 4.1 %collective-permute-done.5 = bf16[2,2,72,320]{3,2,1,0:T(8,128)(2,1)S(1)} collective-permute-done((bf16[2,2,72,320]{3,2,1,0:T(8,128)(2,1)S(1)}, bf16[2,2,72,320]{3,2,1,0:T(8,128)(2,1)S(1)}, u32[]{:S(2)}, u32[]{:S(2)}) %collective-permute-start.5) | collective-permute-done | bytes 184352 | tf_op jit(solution)/shard_map/ppermute | solution.py:15
  56.8 2.9 %collective-permute-start.6 = (bf16[2,1,72,320]{3,2,1,0:T(8,128)(2,1)S(1)}, bf16[2,1,72,320]{3,2,1,0:T(8,128)(2,1)S(1)}, u32[]{:S(2)}, u32[]{:S(2)}) collective-permute-start(bf16[2,1,72,320]{3,2,1,0:T(8,128)(2,1)S(1)} %get-tuple-element.63), channel_id=1, source_target_pairs={{0,1},{1,2},{2,3},{3,4},{4,5},{5,6},{6,7},{7,8},{8,9},{9,10},{10,1... | collective-permute-start | bytes 276488 | tf_op jit(solution)/shard_map/ppermute | solution.py:25
  59.6 2.1 %collective-permute-start.7 = (bf16[2,1,72,320]{3,2,1,0:T(8,128)(2,1)S(1)}, bf16[2,1,72,320]{3,2,1,0:T(8,128)(2,1)S(1)}, u32[]{:S(2)}, u32[]{:S(2)}) collective-permute-start(bf16[2,1,72,320]{3,2,1,0:T(8,128)(2,1)S(1)} %get-tuple-element.64), channel_id=1, source_target_pairs={{1,0},{2,1},{3,2},{4,3},{5,4},{6,5},{7,6},{8,7},{9,8},{10,9},{11,1... | collective-permute-start | bytes 276488 | tf_op jit(solution)/shard_map/ppermute | solution.py:26
  61.8 7.2 %collective-permute-done.7 = bf16[2,1,72,320]{3,2,1,0:T(8,128)(2,1)S(1)} collective-permute-done((bf16[2,1,72,320]{3,2,1,0:T(8,128)(2,1)S(1)}, bf16[2,1,72,320]{3,2,1,0:T(8,128)(2,1)S(1)}, u32[]{:S(2)}, u32[]{:S(2)}) %collective-permute-start.7) | collective-permute-done | bytes 92192 | tf_op jit(solution)/shard_map/ppermute | solution.py:26
  69.9 1.1 %copy-done.2 = bf16[3,3,320,320]{3,2,1,0:T(8,128)(2,1)S(1)} copy-done((bf16[3,3,320,320]{3,2,1,0:T(8,128)(2,1)S(1)}, bf16[3,3,320,320]{3,2,1,0:T(8,128)(2,1)}, u32[]{:S(2)}) %copy-start.2) | copy-done | bytes 1843224
  71.6 0.3 convolution_add_fusion.19
  72.9 0.3 convolution_add_fusion.15
  73.5 0.4 multiply_convert_fusion.1
  74.6 0.3 fusion.6
  75.0 1.9 %collective-permute-start.8 = (bf16[2,1,72,320]{3,2,1,0:T(8,128)(2,1)S(1)}, bf16[2,1,72,320]{3,2,1,0:T(8,128)(2,1)S(1)}, u32[]{:S(2)}, u32[]{:S(2)}) collective-permute-start(bf16[2,1,72,320]{3,2,1,0:T(8,128)(2,1)S(1)} %get-tuple-element.59), channel_id=1, source_target_pairs={{0,1},{1,2},{2,3},{3,4},{4,5},{5,6},{6,7},{7,8},{8,9},{9,10},{10,1... | collective-permute-start | bytes 276488 | tf_op jit(solution)/shard_map/ppermute | solution.py:25
  76.9 2.4 %collective-permute-start.9 = (bf16[2,1,72,320]{3,2,1,0:T(8,128)(2,1)S(1)}, bf16[2,1,72,320]{3,2,1,0:T(8,128)(2,1)S(1)}, u32[]{:S(2)}, u32[]{:S(2)}) collective-permute-start(bf16[2,1,72,320]{3,2,1,0:T(8,128)(2,1)S(1)} %get-tuple-element.60), channel_id=1, source_target_pairs={{1,0},{2,1},{3,2},{4,3},{5,4},{6,5},{7,6},{8,7},{9,8},{10,9},{11,1... | collective-permute-start | bytes 276488 | tf_op jit(solution)/shard_map/ppermute | solution.py:26
  79.3 7.0 %collective-permute-done.9 = bf16[2,1,72,320]{3,2,1,0:T(8,128)(2,1)S(1)} collective-permute-done((bf16[2,1,72,320]{3,2,1,0:T(8,128)(2,1)S(1)}, bf16[2,1,72,320]{3,2,1,0:T(8,128)(2,1)S(1)}, u32[]{:S(2)}, u32[]{:S(2)}) %collective-permute-start.9) | collective-permute-done | bytes 92192 | tf_op jit(solution)/shard_map/ppermute | solution.py:26
  87.1 0.3 convolution_add_fusion.10
  88.0 0.3 convolution_add_fusion.7
  88.7 0.3 convolution_add_fusion.5
  89.3 0.3 convolution_add_fusion.3
  89.6 0.4 multiply_convert_fusion
  90.4 0.3 convolution_add_fusion.1
  90.7 0.3 fusion.8
  91.1 1.0 %select_n.53 = bf16[1,2,2,23040]{3,2,1,0:T(2,128)(2,1)} reshape(bf16[288,320]{1,0:T(8,128)(2,1)S(1)} %fusion.8) | data formatting | bytes 368640 | tf_op jit(solution)/shard_map/jit(_where)/select_n | solution.py:102
  (82 shorter events, 12.2 us)
Async XLA Ops:
  0.0 6.0 %copy-start = (f32[1,2,320,320]{3,2,1,0:T(8,128)S(1)}, f32[1,2,320,320]{3,2,1,0:T(8,128)}, u32[]{:S(2)}) copy-start(f32[1,2,320,320]{3,2,1,0:T(8,128)} %param.13) | copy-start | bytes 2457604
  1.9 8.9 %collective-permute-start = (bf16[2,2,72,320]{3,2,1,0:T(8,128)(2,1)}, bf16[2,2,72,320]{3,2,1,0:T(8,128)(2,1)S(1)}, u32[]{:S(2)}, u32[]{:S(2)}) collective-permute-start(bf16[2,2,72,320]{3,2,1,0:T(8,128)(2,1)} %reshape.267), channel_id=1, source_target_pairs={{0,64},{64,128},{128,192},{192,0},{1,65},{65,129},{129,193},{193,1... | collective-permute-start | bytes 552968 | tf_op jit(solution)/shard_map/ppermute | solution.py:15
  6.6 4.2 %copy-start.5 = (f32[1,2,320]{2,1,0:T(2,128)S(1)}, f32[1,2,320]{2,1,0:T(2,128)}, u32[]{:S(2)}) copy-start(f32[1,2,320]{2,1,0:T(2,128)} %param.10) | copy-start | bytes 7684
  10.8 7.5 %collective-permute-start.1 = (bf16[2,1,72,320]{3,2,1,0:T(8,128)(2,1)S(1)}, bf16[2,1,72,320]{3,2,1,0:T(8,128)(2,1)S(1)}, u32[]{:S(2)}, u32[]{:S(2)}) collective-permute-start(bf16[2,1,72,320]{3,2,1,0:T(8,128)(2,1)S(1)} %get-tuple-element.71), channel_id=1, source_target_pairs={{0,1},{1,2},{2,3},{3,4},{4,5},{5,6},{6,7},{7,8},{8,9},{9,10},{10,1... | collective-permute-start | bytes 276488 | tf_op jit(solution)/shard_map/ppermute | solution.py:25
  16.3 9.4 %collective-permute-start.2 = (bf16[2,1,72,320]{3,2,1,0:T(8,128)(2,1)S(1)}, bf16[2,1,72,320]{3,2,1,0:T(8,128)(2,1)S(1)}, u32[]{:S(2)}, u32[]{:S(2)}) collective-permute-start(bf16[2,1,72,320]{3,2,1,0:T(8,128)(2,1)S(1)} %get-tuple-element.72), channel_id=1, source_target_pairs={{1,0},{2,1},{3,2},{4,3},{5,4},{6,5},{7,6},{8,7},{9,8},{10,9},{11,1... | collective-permute-start | bytes 276488 | tf_op jit(solution)/shard_map/ppermute | solution.py:26
  26.0 1.6 %copy-start.1 = (bf16[3,3,320,320]{3,2,1,0:T(8,128)(2,1)S(1)}, bf16[3,3,320,320]{3,2,1,0:T(8,128)(2,1)}, u32[]{:S(2)}) copy-start(bf16[3,3,320,320]{3,2,1,0:T(8,128)(2,1)} %get-tuple-element.20) | copy-start | bytes 5529604
  29.9 1.4 %copy-start.3 = (bf16[1,2,3,320,320]{4,3,2,1,0:T(8,128)(2,1)S(1)}, bf16[1,2,3,320,320]{4,3,2,1,0:T(8,128)(2,1)}, u32[]{:S(2)}) copy-start(bf16[1,2,3,320,320]{4,3,2,1,0:T(8,128)(2,1)} %param.12) | copy-start | bytes 3686404
  31.3 6.0 %copy-start.6 = (s32[5]{0:T(128)S(1)}, s32[5]{0:T(128)}, u32[]{:S(2)}) copy-start(s32[5]{0:T(128)} %param.8) | copy-start | bytes 64
  32.9 6.4 %collective-permute-start.3 = (bf16[2,1,72,320]{3,2,1,0:T(8,128)(2,1)}, bf16[2,1,72,320]{3,2,1,0:T(8,128)(2,1)}, u32[]{:S(2)}, u32[]{:S(2)}) collective-permute-start(bf16[2,1,72,320]{3,2,1,0:T(8,128)(2,1)} %get-tuple-element.67), channel_id=1, source_target_pairs={{0,1},{1,2},{2,3},{3,4},{4,5},{5,6},{6,7},{7,8},{8,9},{9,10},{10,1... | collective-permute-start | bytes 276488 | tf_op jit(solution)/shard_map/ppermute | solution.py:25
  34.8 9.5 %collective-permute-start.4 = (bf16[2,1,72,320]{3,2,1,0:T(8,128)(2,1)S(1)}, bf16[2,1,72,320]{3,2,1,0:T(8,128)(2,1)}, u32[]{:S(2)}, u32[]{:S(2)}) collective-permute-start(bf16[2,1,72,320]{3,2,1,0:T(8,128)(2,1)S(1)} %get-tuple-element.68), channel_id=1, source_target_pairs={{1,0},{2,1},{3,2},{4,3},{5,4},{6,5},{7,6},{8,7},{9,8},{10,9},{11,1... | collective-permute-start | bytes 276488 | tf_op jit(solution)/shard_map/ppermute | solution.py:26
  48.3 1.4 %copy-start.4 = (bf16[1,2,3,320,320]{4,3,2,1,0:T(8,128)(2,1)S(1)}, bf16[1,2,3,320,320]{4,3,2,1,0:T(8,128)(2,1)}, u32[]{:S(2)}) copy-start(bf16[1,2,3,320,320]{4,3,2,1,0:T(8,128)(2,1)} %param.12) | copy-start | bytes 3686404
  50.7 6.1 %collective-permute-start.5 = (bf16[2,2,72,320]{3,2,1,0:T(8,128)(2,1)S(1)}, bf16[2,2,72,320]{3,2,1,0:T(8,128)(2,1)S(1)}, u32[]{:S(2)}, u32[]{:S(2)}) collective-permute-start(bf16[2,2,72,320]{3,2,1,0:T(8,128)(2,1)S(1)} %broadcast_select_fusion), channel_id=1, source_target_pairs={{0,64},{64,128},{128,192},{192,0},{1,65},{65,129},{129,193},{193,1... | collective-permute-start | bytes 552968 | tf_op jit(solution)/shard_map/ppermute | solution.py:15
  56.8 5.0 %collective-permute-start.6 = (bf16[2,1,72,320]{3,2,1,0:T(8,128)(2,1)S(1)}, bf16[2,1,72,320]{3,2,1,0:T(8,128)(2,1)S(1)}, u32[]{:S(2)}, u32[]{:S(2)}) collective-permute-start(bf16[2,1,72,320]{3,2,1,0:T(8,128)(2,1)S(1)} %get-tuple-element.63), channel_id=1, source_target_pairs={{0,1},{1,2},{2,3},{3,4},{4,5},{5,6},{6,7},{7,8},{8,9},{9,10},{10,1... | collective-permute-start | bytes 276488 | tf_op jit(solution)/shard_map/ppermute | solution.py:25
  59.6 9.4 %collective-permute-start.7 = (bf16[2,1,72,320]{3,2,1,0:T(8,128)(2,1)S(1)}, bf16[2,1,72,320]{3,2,1,0:T(8,128)(2,1)S(1)}, u32[]{:S(2)}, u32[]{:S(2)}) collective-permute-start(bf16[2,1,72,320]{3,2,1,0:T(8,128)(2,1)S(1)} %get-tuple-element.64), channel_id=1, source_target_pairs={{1,0},{2,1},{3,2},{4,3},{5,4},{6,5},{7,6},{8,7},{9,8},{10,9},{11,1... | collective-permute-start | bytes 276488 | tf_op jit(solution)/shard_map/ppermute | solution.py:26
  69.4 1.6 %copy-start.2 = (bf16[3,3,320,320]{3,2,1,0:T(8,128)(2,1)S(1)}, bf16[3,3,320,320]{3,2,1,0:T(8,128)(2,1)}, u32[]{:S(2)}) copy-start(bf16[3,3,320,320]{3,2,1,0:T(8,128)(2,1)} %get-tuple-element.20) | copy-start | bytes 5529604
  75.0 4.3 %collective-permute-start.8 = (bf16[2,1,72,320]{3,2,1,0:T(8,128)(2,1)S(1)}, bf16[2,1,72,320]{3,2,1,0:T(8,128)(2,1)S(1)}, u32[]{:S(2)}, u32[]{:S(2)}) collective-permute-start(bf16[2,1,72,320]{3,2,1,0:T(8,128)(2,1)S(1)} %get-tuple-element.59), channel_id=1, source_target_pairs={{0,1},{1,2},{2,3},{3,4},{4,5},{5,6},{6,7},{7,8},{8,9},{9,10},{10,1... | collective-permute-start | bytes 276488 | tf_op jit(solution)/shard_map/ppermute | solution.py:25
  76.9 9.4 %collective-permute-start.9 = (bf16[2,1,72,320]{3,2,1,0:T(8,128)(2,1)S(1)}, bf16[2,1,72,320]{3,2,1,0:T(8,128)(2,1)S(1)}, u32[]{:S(2)}, u32[]{:S(2)}) collective-permute-start(bf16[2,1,72,320]{3,2,1,0:T(8,128)(2,1)S(1)} %get-tuple-element.60), channel_id=1, source_target_pairs={{1,0},{2,1},{3,2},{4,3},{5,4},{6,5},{7,6},{8,7},{9,8},{10,9},{11,1... | collective-permute-start | bytes 276488 | tf_op jit(solution)/shard_map/ppermute | solution.py:26
where the time goes:
time: 92.5 us; the launch traced here: 92 us
  waiting for transfers between devices  30.8 us (33%)
  starting transfers between devices  23.7 us (26%)
  matrix products  16.4 us (18%)
  local copies, waits for them, and re-layouts  14.7 us (16%)
  between operations  3.26 us (4%)
  other arithmetic  3.21 us (3%)
    ppermute x4, waiting for transfers between devices, with_halo(): after = lax.ppermute(initial, axis, down)  26.6 us
    ppermute x4, starting transfers between devices, with_halo(): before = lax.ppermute(last, axis, up)  12.2 us
    dot_general x36, matrix products, block_rows(): jnp.dot(window, spatial[shift_y, shift_x], preferred_element_type=jnp.flo...  11.5 us
    ppermute x4, starting transfers between devices, with_halo(): after = lax.ppermute(initial, axis, down)  8.84 us
    ppermute x2, waiting for transfers between devices, from_behind(): lax.ppermute(value, axis, [(i, (i + by) % length) for i in range(length)])  4.13 us
    squeeze x1, local copies, waits for them, and re-layouts, apply(): spatial_weight[0, slot]  4.1 us
    dot_general x12, matrix products, block_rows(): jnp.dot(framed[tap:tap + frames].reshape(-1, chans), temporal[tap], prefe...  3.82 us
    unnamed x14, local copies, waits for them, and re-layouts  3.53 us
  transfers between devices with their start and end apart: 10, of which 5 were waited for; matrix products, arithmetic and copies ran while one was open for 8% of the time, Pallas kernels for 0%

commit v1 on v0

v1 whole, which is shorter than its diff:
```python
import math

import jax
import jax.numpy as jnp
from jax import lax
from jax.experimental import pallas as pl
from jax.experimental.pallas import tpu as pltpu
from jax.sharding import PartitionSpec as P

C = 320
W = 72
STEPS = 2
FRAMES = 2
SEGMENTS = 4
GROUPS = 64
MAIN = 256
REST = C - MAIN
PIX = FRAMES * W
PACK = 2 * MAIN + 2 * REST
NOUT = 4 * MAIN
MESH = pl.DeviceIdType.MESH
F32 = jnp.float32
BF16 = jnp.bfloat16


def lanes(shape):
    return lax.broadcasted_iota(jnp.int32, shape, len(shape) - 1)


def roll_rest(value):
    return pltpu.roll(value, REST, 1)


def norm_pair(pair, gain_main, gain_rest, xm, xr, at):
    main_a = pair[:, :MAIN].astype(F32)
    main_b = pair[:, MAIN : 2 * MAIN].astype(F32)
    rest = pair[:, 2 * MAIN :].astype(F32)
    low = lanes(rest.shape) < REST
    square = rest * rest
    zero = jnp.zeros_like(square)

    def scale(main, own):
        both = main * main
        total = both[:, :128] + both[:, 128:] + own
        return lax.rsqrt(jnp.sum(total, axis=-1, keepdims=True) * (1.0 / C) + 1e-06)

    scale_a = scale(main_a, jnp.where(low, square, zero))
    scale_b = scale(main_b, jnp.where(low, zero, square))
    xm[2 * at] = (main_a * scale_a * gain_main).astype(BF16)
    xm[2 * at + 1] = (main_b * scale_b * gain_main).astype(BF16)
    xr[at] = (rest * jnp.where(low, scale_a, scale_b) * gain_rest).astype(BF16)


def block(xm, xr, at, pair_a, pair_b, wm, wr, wt, slot, bias_main, bias_rest):
    left = jnp.concatenate([xm[pl.ds(2 * at + dy, 2)].reshape(2 * PIX, MAIN) for dy in range(3)], axis=1)
    left_rest = jnp.concatenate([xr[at], xr[at + 1]], axis=1)
    spot = lax.rem(lax.broadcasted_iota(jnp.int32, (2 * PIX, 1), 0), W)
    first, last = spot == 0, spot == W - 1

    def product(tile):
        cols = slice(tile * MAIN, (tile + 1) * MAIN)
        main = jnp.dot(left, wm[slot, :, cols], preferred_element_type=F32)
        rest = [jnp.dot(left_rest, wr[slot, row, :, cols], preferred_element_type=F32) for row in range(2)]
        return main + jnp.concatenate(rest, axis=0)

    def from_before(value):
        return jnp.where(first, 0.0, pltpu.roll(value, 1, 0))

    def from_after(value):
        return jnp.where(last, 0.0, pltpu.roll(value, value.shape[0] - 1, 0))

    a_main = from_before(product(0)) + product(1) + from_after(product(2)) + bias_main
    z = product(3)
    sides = from_before(z[:, :128]) + from_after(z[:, 128:])
    centre = z[:, :128]
    low = lanes((PIX, 128)) < REST
    a_rest = jnp.where(
        low,
        sides[:PIX] + roll_rest(centre[:PIX]),
        roll_rest(sides[PIX:]) + centre[PIX:],
    ) + bias_rest

    def silu(value):
        return value * (0.5 * jnp.tanh(0.5 * value) + 0.5)

    u_main = silu(a_main)
    u_rest = silu(a_rest)
    low = lanes((W, 128)) < REST

    def transposed(first_half, second_half):
        return (
            jnp.where(low, first_half, roll_rest(second_half)),
            jnp.where(low, roll_rest(first_half), second_half),
        )

    rest_a, rest_b = transposed(u_rest[:W], u_rest[W:])
    mixed = jnp.concatenate(
        [
            jnp.concatenate([u_main[:W], u_main[PIX : PIX + W]], axis=0),
            jnp.concatenate([u_main[W:PIX], u_main[PIX + W :]], axis=0),
            jnp.concatenate([rest_a, rest_b], axis=0),
        ],
        axis=1,
    ).astype(BF16)
    v = jnp.dot(mixed, wt[slot], preferred_element_type=F32)
    v_a = jnp.concatenate([v[:W, :MAIN], v[:W, MAIN : 2 * MAIN]], axis=0)
    v_b = jnp.concatenate([v[W:, :MAIN], v[W:, MAIN : 2 * MAIN]], axis=0)
    v_rest = jnp.concatenate(transposed(v[:W, 2 * MAIN :], v[W:, 2 * MAIN :]), axis=0)
    low = lanes((PIX, 128)) < REST
    h_a = pair_a[:, MAIN : 2 * MAIN].astype(F32)
    h_b = pair_b[:, :MAIN].astype(F32)
    h_rest = roll_rest(jnp.where(low, pair_b[:, 2 * MAIN :].astype(F32), pair_a[:, 2 * MAIN :].astype(F32)))
    return h_a + a_main[:PIX] + v_a, h_b + a_main[PIX:] + v_b, h_rest + a_rest + v_rest


def kernel(
    state, bounds, timesteps, gains, spatial, temporal, time_weight,
    out,
    raw_s, raw_t, raw_b, wm, wr, wt, packed, arrived, hidden, xm, xr, hm, hr,
    load_sem, send_sem, recv_sem,
):
    segment = lax.axis_index("segment")
    group = lax.axis_index("rows")
    core = lax.rem(group, 2)
    behind, ahead = lax.rem(segment + SEGMENTS - 1, SEGMENTS), lax.rem(segment + 1, SEGMENTS)
    across = group - 1 + 2 * core
    inner = group + 1 - 2 * core
    has_across = (across >= 0) & (across < GROUPS)

    loads = []
    for slot in range(2):
        loads.append(
            (
                pltpu.make_async_copy(spatial.at[slot], raw_s.at[slot], load_sem.at[slot, 0]),
                pltpu.make_async_copy(temporal.at[slot], raw_t.at[slot], load_sem.at[slot, 1]),
                pltpu.make_async_copy(time_weight.at[slot], raw_b.at[slot], load_sem.at[slot, 2]),
            )
        )
        for load in loads[-1]:
            load.start()

    barrier = pltpu.get_barrier_semaphore()
    pl.semaphore_signal(barrier, inc=1, device_id=(behind, group), device_id_type=MESH)
    pl.semaphore_signal(barrier, inc=1, device_id=(segment, inner), device_id_type=MESH)

    @pl.when(has_across)
    def _():
        pl.semaphore_signal(barrier, inc=1, device_id=(behind, across), device_id_type=MESH)

    rows = [[state[f, row].astype(F32) for f in range(FRAMES)] for row in range(2)]
    main = [jnp.concatenate([x[:, :MAIN] for x in row], axis=0) for row in rows]
    rest = [jnp.concatenate([x[:, MAIN:] for x in row], axis=0) for row in rows]
    packed[0] = jnp.concatenate(main + rest, axis=1).astype(BF16)

    pl.semaphore_wait(barrier, 2 + has_across.astype(jnp.int32))

    def own_copy(step):
        return pltpu.make_async_remote_copy(
            packed.at[step], arrived.at[step, 1], send_sem.at[step, 0], recv_sem.at[step, 0],
            device_id=(ahead, group), device_id_type=MESH,
        )

    def across_copy(step):
        return pltpu.make_async_remote_copy(
            packed.at[step], arrived.at[step, 2 - 2 * core], send_sem.at[step, 1], recv_sem.at[step, 1],
            device_id=(ahead, across), device_id_type=MESH,
        )

    def inner_copy(step):
        return pltpu.make_async_remote_copy(
            arrived.at[step, 1], arrived.at[step, 2 * core], send_sem.at[step, 2], recv_sem.at[step, 2],
            device_id=(segment, inner), device_id_type=MESH,
        )

    def send(step):
        own_copy(step).start()

        @pl.when(has_across)
        def _():
            across_copy(step).start()

    send(0)

    for slot in range(2):
        for load in loads[slot]:
            load.wait()
        for dy in range(3):
            for dx in range(3):
                wm[slot, dy * MAIN : (dy + 1) * MAIN, dx * MAIN : (dx + 1) * MAIN] = raw_s[slot, 3 * dy + dx, :MAIN, :MAIN]
                for row in range(2):
                    at = (dy + row) * REST
                    wr[slot, row, at : at + REST, dx * MAIN : (dx + 1) * MAIN] = raw_s[slot, 3 * dy + dx, MAIN:, :MAIN]
            rests = [raw_s[slot, 3 * dy + dx, :, MAIN:] for dx in range(3)]
            rests = jnp.concatenate(rests + [jnp.zeros_like(rests[0])], axis=1)
            wm[slot, dy * MAIN : (dy + 1) * MAIN, 3 * MAIN :] = rests[:MAIN]
            for row in range(2):
                at = (dy + row) * REST
                wr[slot, row, at : at + REST, 3 * MAIN :] = rests[MAIN:]
        wr[slot, 0, 3 * REST :] = jnp.zeros((REST, NOUT), BF16)
        wr[slot, 1, :REST] = jnp.zeros((REST, NOUT), BF16)
        for f in range(FRAMES):
            for g in range(FRAMES):
                tap = f - g + 1
                wt[slot, f * MAIN : (f + 1) * MAIN, g * MAIN : (g + 1) * MAIN] = raw_t[slot, tap, :MAIN, :MAIN]
                at = 2 * MAIN + f * REST
                wt[slot, at : at + REST, g * MAIN : (g + 1) * MAIN] = raw_t[slot, tap, MAIN:, :MAIN]
            rests = jnp.concatenate([raw_t[slot, f - g + 1, :, MAIN:] for g in range(FRAMES)], axis=1)
            wt[slot, f * MAIN : (f + 1) * MAIN, 2 * MAIN :] = rests[:MAIN]
            at = 2 * MAIN + f * REST
            wt[slot, at : at + REST, 2 * MAIN :] = rests[MAIN:]

    half = C // 2
    number = lax.broadcasted_iota(jnp.int32, (8, half), 1).astype(F32)
    which = lax.broadcasted_iota(jnp.int32, (8, half), 0)
    t = jnp.where(which == 0, timesteps[0], timesteps[1]).astype(F32)
    angle = t * jnp.exp(-math.log(10000.0) * number / half)
    emb = jnp.concatenate([jnp.cos(angle), jnp.sin(angle)], axis=1)
    bias = [
        jnp.dot(emb, raw_b[slot], preferred_element_type=F32, precision=lax.Precision.HIGHEST) for slot in range(2)
    ]

    def twice(value):
        return jnp.concatenate([value, value], axis=1)

    gain_main = [gains[slot : slot + 1, :MAIN] for slot in range(2)]
    gain_rest = [twice(gains[slot : slot + 1, MAIN:]) for slot in range(2)]
    two = jnp.full((1, 128), bounds[segment + 1] - bounds[segment], jnp.int32) > 1
    two_main = jnp.concatenate([two, two], axis=1)

    for step in range(STEPS):
        bias_main = [bias[slot][step : step + 1, :MAIN] for slot in range(2)]
        bias_rest = [twice(bias[slot][step : step + 1, MAIN:]) for slot in range(2)]

        def norm(at, step=step):
            norm_pair(arrived[step, at], gain_main[0], gain_rest[0], xm, xr, at)

        def first_block(at, step=step, bias_main=bias_main, bias_rest=bias_rest):
            main_a, main_b, rest = block(
                xm, xr, at, arrived[step, at], arrived[step, at + 1], wm, wr, wt, 0, bias_main[0], bias_rest[0]
            )
            row_a = 2 * group - 1 + 2 * at
            inside_a, inside_b = row_a >= 0, row_a + 1 < 2 * GROUPS
            low = lanes(rest.shape) < REST
            main_a = jnp.where(inside_a, main_a, 0.0)
            main_b = jnp.where(inside_b, main_b, 0.0)
            rest = jnp.where(low, jnp.where(inside_a, rest, 0.0), jnp.where(inside_b, rest, 0.0))
            hidden[at] = jnp.concatenate([main_a, main_b, rest], axis=1).astype(BF16)
            norm_pair(hidden[at], gain_main[1], gain_rest[1], hm, hr, at)

        own_copy(step).wait_recv()
        inner_copy(step).start()
        norm(1)
        inner_copy(step).wait_recv()
        near = 2 - 2 * core
        norm(near)
        first_block(1 - core)

        @pl.when(has_across)
        def _(step=step):
            across_copy(step).wait_recv()

        @pl.when(jnp.logical_not(has_across))
        def _(step=step):
            arrived[step, 2 * core] = jnp.zeros((PIX, PACK), BF16)

        norm(2 - near)
        first_block(core)
        main_a, main_b, rest = block(
            hm, hr, 0, hidden[0], hidden[1], wm, wr, wt, 1, bias_main[1], bias_rest[1]
        )
        h_a = hidden[0][:, MAIN : 2 * MAIN].astype(F32)
        h_b = hidden[1][:, :MAIN].astype(F32)
        low = lanes((PIX, 128)) < REST
        h_rest = roll_rest(jnp.where(low, hidden[1][:, 2 * MAIN :].astype(F32), hidden[0][:, 2 * MAIN :].astype(F32)))
        main_a = jnp.where(two_main, main_a, h_a)
        main_b = jnp.where(two_main, main_b, h_b)
        rest = jnp.where(two, rest, h_rest)
        if step + 1 < STEPS:
            packed[step + 1] = jnp.concatenate([main_a, main_b, rest], axis=1).astype(BF16)
            send(step + 1)
        else:
            for row, main in enumerate((main_a, main_b)):
                for f in range(FRAMES):
                    spot = slice(f * W, (f + 1) * W)
                    own = rest[spot, row * REST : (row + 1) * REST]
                    out[f, row] = jnp.concatenate([main[spot], own], axis=1).astype(BF16)

    for step in range(STEPS):
        own_copy(step).wait_send()
        inner_copy(step).wait_send()

        @pl.when(has_across)
        def _(step=step):
            across_copy(step).wait_send()


def body(state, bounds, timesteps, gains, spatial_weight, temporal_weight, time_weight):
    vmem = pl.BlockSpec(memory_space=pltpu.VMEM)
    smem = pl.BlockSpec(memory_space=pltpu.SMEM)
    hbm = pl.BlockSpec(memory_space=pl.ANY)
    out = pl.pallas_call(
        kernel,
        out_shape=jax.ShapeDtypeStruct((FRAMES, 2, W, C), BF16),
        in_specs=[vmem, smem, smem, vmem, hbm, hbm, hbm],
        out_specs=vmem,
        scratch_shapes=[
            pltpu.VMEM((2, 9, C, C), BF16),
            pltpu.VMEM((2, 3, C, C), BF16),
            pltpu.VMEM((2, C, C), F32),
            pltpu.VMEM((2, 3 * MAIN, NOUT), BF16),
            pltpu.VMEM((2, 2, MAIN, NOUT), BF16),
            pltpu.VMEM((2, PACK, PACK), BF16),
            pltpu.VMEM((STEPS, PIX, PACK), BF16),
            pltpu.VMEM((STEPS, 3, PIX, PACK), BF16),
            pltpu.VMEM((2, PIX, PACK), BF16),
            pltpu.VMEM((6, PIX, MAIN), BF16),
            pltpu.VMEM((3, PIX, 128), BF16),
            pltpu.VMEM((4, PIX, MAIN), BF16),
            pltpu.VMEM((2, PIX, 128), BF16),
            pltpu.SemaphoreType.DMA((2, 3)),
            pltpu.SemaphoreType.DMA((STEPS, 3)),
            pltpu.SemaphoreType.DMA((STEPS, 3)),
        ],
        compiler_params=pltpu.CompilerParams(
            collective_id=1, has_side_effects=True, vmem_limit_bytes=56 << 20
        ),
        cost_estimate=pl.CostEstimate(flops=4 << 30, bytes_accessed=6 << 20, transcendentals=1 << 20),
        name="cycle",
    )(
        state.reshape(FRAMES, 2, W, C),
        bounds,
        timesteps,
        gains.reshape(2, C),
        spatial_weight.reshape(2, 9, C, C),
        temporal_weight.reshape(2, 3, C, C),
        time_weight.reshape(2, C, C),
    )
    return out.reshape(1, FRAMES, 2, W * C)


def solution(mesh):
    placed = (
        P("segment", None, "rows", None),
        P(),
        P(),
        P("segment", None, None),
        P("segment", None, None, None, None, None),
        P("segment", None, None, None, None),
        P("segment", None, None, None),
    )
    return jax.shard_map(
        body,
        mesh=mesh,
        in_specs=placed,
        out_specs=P("segment", None, "rows", None),
        check_vma=False,
    )
```

time: 92.5 us -> 40.6 us (0.44)
  Pallas kernels: 0 us -> 36.4 us
  waiting for transfers between devices: 30.8 us -> 0 us
  starting transfers between devices: 23.7 us -> 0 us
  matrix products: 16.4 us -> 0 us
  local copies, waits for them, and re-layouts: 14.7 us -> 3.72 us
  between operations: 3.26 us -> 0.01 us
  other arithmetic: 3.21 us -> 0 us
    pallas_call x0 -> x1, Pallas kernels: none -> 36.4 us  [body(): pl.pallas_call(kernel, out_shape=jax.ShapeDtypeStruct((FRAMES, 2, W, C),...]
    ppermute x10 -> x0, waiting for transfers between devices: 30.8 us -> none  [the longest x4 26.6 us: with_halo(): after = lax.ppermute(initial, axis, down)]
    ppermute x10 -> x0, starting transfers between devices: 23.7 us -> none  [the longest x4 12.2 us: with_halo(): before = lax.ppermute(last, axis, up)]
    dot_general x50 -> x0, matrix products: 16.4 us -> none  [the longest x36 11.5 us: block_rows(): jnp.dot(window, spatial[shift_y, shift_x], preferred_element_type=jnp.flo...]
    squeeze x1 -> x0, local copies, waits for them, and re-layouts: 4.1 us -> none  [apply(): spatial_weight[0, slot]]
    unnamed x14 -> x0, local copies, waits for them, and re-layouts: 3.53 us -> none
    slice x20 -> x0, local copies, waits for them, and re-layouts: 3.49 us -> none  [the longest x1 1.31 us: body(): emb = embed(timesteps[step], time_weight.shape[2])]
    reduce_sum x4 -> x0, other arithmetic: 2.18 us -> none  [block_rows(): scale = lax.rsqrt(jnp.mean(values * values, axis=-1, keepdims=True) + 1e-06)]
  transfers between devices with their start and end apart: 10 -> 0, of which waited for: 5 -> 0; matrix products, arithmetic and copies ran while one was open for 8% -> 0% of each run, Pallas kernels for 0% -> 0%
where the time goes in v1:
time: 40.6 us; the launch traced here: 40.1 us
  Pallas kernels  36.4 us (90%)
  local copies, waits for them, and re-layouts  3.72 us (9%)
    pallas_call x1, Pallas kernels, body(): pl.pallas_call(kernel, out_shape=jax.ShapeDtypeStruct((FRAMES, 2, W, C),...  36.4 us
    reshape x1, local copies, waits for them, and re-layouts, body(): return out.reshape(1, FRAMES, 2, W * C)  1.89 us
    reshape x1, local copies, waits for them, and re-layouts, body(): state.reshape(FRAMES, 2, W, C)  1.83 us

profile of v1, /device:TPU:103, one launch (start us, length us, event | category | flops | bytes accessed | tf_op | source)
XLA Modules:
  0.0 40.1 jit_solution(11208718428486486518)
XLA Ops:
  0.0 1.8 %reshape.18.state = bf16[2,2,72,320]{3,2,1,0:T(8,128)(2,1)} reshape(bf16[1,2,2,23040]{3,2,1,0:T(2,128)(2,1)} %param.7) | data formatting | bytes 368640 | tf_op jit(solution)/shard_map/reshape | solution.py:330
  1.8 36.4 %cycle.1 = bf16[2,2,72,320]{3,2,1,0:T(8,128)(2,1)} custom-call(bf16[2,2,72,320]{3,2,1,0:T(8,128)(2,1)} %reshape.18.state, s32[5]{0:T(128)} %bounds.1, s32[2]{0:T(128)} %timesteps.1, f32[2,320]{1,0:T(2,128)} %bitcast.9, bf16[2,9,320,320]{3,2,1,0:T(8,128)(2,1)} %bitcast.6, bf16[2,3,320,320]{3,2,1,0:T(8,128)(2,1)} %bitcast.7, f32[2,320,320]{2,1,0:T(8,128)} %bitcast.8), custom_call_target="tpu_custom_call" | custom-call | flops 4294967296 | bytes 6291456 | tf_op jit(solution)/shard_map/cycle/pallas_call | solution.py:301
  38.2 1.9 %reshape.23 = bf16[1,2,2,23040]{3,2,1,0:T(2,128)(2,1)} reshape(bf16[2,2,72,320]{3,2,1,0:T(8,128)(2,1)} %cycle.1) | data formatting | bytes 368640 | tf_op jit(solution)/shard_map/reshape | solution.py:338

commit v2 on v1

v2 whole, which is shorter than its diff:
```python
import math

import jax
import jax.numpy as jnp
from jax import lax
from jax.experimental import pallas as pl
from jax.experimental.pallas import tpu as pltpu
from jax.sharding import PartitionSpec as P

C = 320
W = 72
STEPS = 2
FRAMES = 2
SEGMENTS = 4
GROUPS = 64
MAIN = 256
REST = C - MAIN
PIX = FRAMES * W
PACK = 2 * MAIN + 2 * REST
NOUT = 4 * MAIN
PARTS = ((0, 48), (48, 48), (96, 48))
NEAR = ((0, 1, None, 2), (None, 0, 2, 1))
AFTER = ((2, None), (1, 2))
BEFORE = ((0, 1), (None, 0))
BEFORE_REVERSED = ((1, 0), (0, None))
MESH = pl.DeviceIdType.MESH
F32 = jnp.float32
BF16 = jnp.bfloat16


def lanes(shape):
    return lax.broadcasted_iota(jnp.int32, shape, len(shape) - 1)


def roll_rest(value):
    return pltpu.roll(value, REST, 1)


def norm_pair(pair, gain_main, gain_rest, xm, xr, first, second, at, spot=slice(None)):
    main_a = pair[:, :MAIN].astype(F32)
    main_b = pair[:, MAIN : 2 * MAIN].astype(F32)
    rest = pair[:, 2 * MAIN :].astype(F32)
    low = lanes(rest.shape) < REST
    square = rest * rest
    zero = jnp.zeros_like(square)

    def scale(main, own):
        both = main * main
        total = both[:, :128] + both[:, 128:] + own
        return lax.rsqrt(jnp.sum(total, axis=-1, keepdims=True) * (1.0 / C) + 1e-06)

    scale_a = scale(main_a, jnp.where(low, square, zero))
    scale_b = scale(main_b, jnp.where(low, zero, square))
    xm[first, spot] = (main_a * scale_a * gain_main).astype(BF16)
    xm[second, spot] = (main_b * scale_b * gain_main).astype(BF16)
    xr[at, spot] = (rest * jnp.where(low, scale_a, scale_b) * gain_rest).astype(BF16)


def dot(left, right):
    return jnp.dot(left, right, preferred_element_type=F32)


def columns(tile):
    return slice(tile * MAIN, (tile + 1) * MAIN)


def before_part(xm, row, rest, wm, wr, tile):
    cols = columns(tile)
    one = dot(jnp.concatenate([xm[row], xm[row + 1]], axis=1), wm[: 2 * MAIN, cols]) + dot(rest, wr[0, :, cols])
    two = dot(xm[row + 1], wm[:MAIN, cols]) + dot(rest, wr[1, :, cols])
    return jnp.concatenate([one, two], axis=0)


def after_part(xm, row, rest, wm, wr, tile):
    cols = columns(tile)
    one = dot(xm[row], wm[2 * MAIN :, cols]) + dot(rest, wr[0, :, cols])
    two = dot(jnp.concatenate([xm[row], xm[row + 1]], axis=1), wm[MAIN:, cols]) + dot(rest, wr[1, :, cols])
    return jnp.concatenate([one, two], axis=0)


def both_parts(xm, row, rest, wm, wr, tile):
    cols = columns(tile)
    left = jnp.concatenate([xm[row + dy : row + dy + 2].reshape(2 * PIX, MAIN) for dy in range(3)], axis=1)
    rests = jnp.concatenate([dot(rest, wr[0, :, cols]), dot(rest, wr[1, :, cols])], axis=0)
    return dot(left, wm[:, cols]) + rests


def finish(product, centre, wt, bias_main, bias_rest):
    spot = lax.rem(lax.broadcasted_iota(jnp.int32, (2 * PIX, 1), 0), W)
    first, last = spot == 0, spot == W - 1

    def from_before(value):
        return jnp.where(first, 0.0, pltpu.roll(value, 1, 0))

    def from_after(value):
        return jnp.where(last, 0.0, pltpu.roll(value, value.shape[0] - 1, 0))

    a_main = from_before(product(0)) + product(1) + from_after(product(2)) + bias_main
    z = product(3)
    sides = from_before(z[:, :128]) + from_after(z[:, 128:])
    middle = z[:, :128]
    low = lanes((PIX, 128)) < REST
    a_rest = jnp.where(
        low,
        sides[:PIX] + roll_rest(middle[:PIX]),
        roll_rest(sides[PIX:]) + middle[PIX:],
    ) + bias_rest

    def silu(value):
        return value * (0.5 * jnp.tanh(0.5 * value) + 0.5)

    u_main = silu(a_main)
    u_rest = silu(a_rest)
    low = lanes((W, 128)) < REST

    def transposed(first_half, second_half):
        return (
            jnp.where(low, first_half, roll_rest(second_half)),
            jnp.where(low, roll_rest(first_half), second_half),
        )

    rest_a, rest_b = transposed(u_rest[:W], u_rest[W:])
    mixed = jnp.concatenate(
        [
            jnp.concatenate([u_main[:W], u_main[PIX : PIX + W]], axis=0),
            jnp.concatenate([u_main[W:PIX], u_main[PIX + W :]], axis=0),
            jnp.concatenate([rest_a, rest_b], axis=0),
        ],
        axis=1,
    ).astype(BF16)
    v = dot(mixed, wt[...])
    v_a = jnp.concatenate([v[:W, :MAIN], v[:W, MAIN : 2 * MAIN]], axis=0)
    v_b = jnp.concatenate([v[W:, :MAIN], v[W:, MAIN : 2 * MAIN]], axis=0)
    v_rest = jnp.concatenate(transposed(v[:W, 2 * MAIN :], v[W:, 2 * MAIN :]), axis=0)
    h_a, h_b, h_rest = centre
    return h_a + a_main[:PIX] + v_a, h_b + a_main[PIX:] + v_b, h_rest + a_rest + v_rest


def kernel(
    state, bounds, timesteps, gains, spatial, temporal, time_weight,
    out,
    raw_s, raw_t, raw_b, wm, w_near, w_own, w_far, w_hid, wt, packed, arrived, hidden, xm, xr, hm, hr, zf, zh,
    load_sem, send_sem, recv_sem,
):
    segment = lax.axis_index("segment")
    group = lax.axis_index("rows")
    core = lax.rem(group, 2)
    behind, ahead = lax.rem(segment + SEGMENTS - 1, SEGMENTS), lax.rem(segment + 1, SEGMENTS)
    across = group - 1 + 2 * core
    inner = group + 1 - 2 * core
    has_across = (across >= 0) & (across < GROUPS)

    loads = []
    for slot in range(2):
        loads.append(
            (
                pltpu.make_async_copy(spatial.at[slot], raw_s.at[slot], load_sem.at[slot, 0]),
                pltpu.make_async_copy(temporal.at[slot], raw_t.at[slot], load_sem.at[slot, 1]),
                pltpu.make_async_copy(time_weight.at[slot], raw_b.at[slot], load_sem.at[slot, 2]),
            )
        )

    barrier = pltpu.get_barrier_semaphore()
    pl.semaphore_signal(barrier, inc=1, device_id=(behind, group), device_id_type=MESH)
    pl.semaphore_signal(barrier, inc=1, device_id=(segment, inner), device_id_type=MESH)

    @pl.when(has_across)
    def _():
        pl.semaphore_signal(barrier, inc=1, device_id=(segment, across), device_id_type=MESH)

    for load in loads[0] + loads[1]:
        load.start()

    rows = [[state[f, row].astype(F32) for f in range(FRAMES)] for row in (core, 1 - core)]
    main = [jnp.concatenate([x[:, :MAIN] for x in row], axis=0) for row in rows]
    rest = [jnp.concatenate([x[:, MAIN:] for x in row], axis=0) for row in rows]
    packed[0] = jnp.concatenate(main + rest, axis=1).astype(BF16)

    pl.semaphore_wait(barrier, 2 + has_across.astype(jnp.int32))

    def piece(step, kind, part, source, target, device):
        spot = pl.ds(*PARTS[part])
        return pltpu.make_async_remote_copy(
            source.at[spot], target.at[spot], send_sem.at[step, kind, part], recv_sem.at[step, kind, part],
            device_id=device, device_id_type=MESH,
        )

    def own_copy(step, part):
        return piece(step, 0, part, packed.at[step], arrived.at[step, 1], (ahead, group))

    def across_copy(step, part):
        return piece(step, 1, part, arrived.at[step, 1], arrived.at[step, 0], (segment, across))

    def inner_copy(step, part):
        return piece(step, 2, part, arrived.at[step, 1], arrived.at[step, 2], (segment, inner))

    parts = range(len(PARTS))
    for part in parts:
        own_copy(0, part).start()

    @pl.when(jnp.logical_not(has_across))
    def _():
        for step in range(STEPS):
            arrived[step, 0] = jnp.zeros((PIX, PACK), BF16)

    none = jnp.zeros((REST, NOUT), BF16)
    for slot in range(2):
        for load in loads[slot]:
            load.wait()
        for dy in range(3):
            taps = [3 * (dy + core * (2 - 2 * dy)) + dx for dx in range(3)]
            for dx in range(3):
                wm[slot, dy * MAIN : (dy + 1) * MAIN, columns(dx)] = raw_s[slot, taps[dx], :MAIN, :MAIN]
            rests = [raw_s[slot, tap, :, MAIN:] for tap in taps]
            rests = jnp.concatenate(rests + [jnp.zeros_like(rests[0])], axis=1)
            wm[slot, dy * MAIN : (dy + 1) * MAIN, columns(3)] = rests[:MAIN]
            tail = jnp.concatenate([raw_s[slot, tap, MAIN:, :MAIN] for tap in taps] + [rests[MAIN:]], axis=1)
            if slot == 0:
                places = ((w_near, NEAR), (w_own, AFTER), (w_far, BEFORE_REVERSED))
            else:
                places = ((w_own, AFTER), (w_hid, BEFORE))
            for ref, order in places:
                ref = ref.at[slot] if ref is w_own else ref
                for row in range(2):
                    for at, tap in enumerate(order[row]):
                        if tap == dy:
                            ref[row, at * REST : (at + 1) * REST] = tail
                        elif tap is None and dy == 0:
                            ref[row, at * REST : (at + 1) * REST] = none
        for f in range(FRAMES):
            for g in range(FRAMES):
                tap = f - g + 1
                wt[slot, f * MAIN : (f + 1) * MAIN, columns(g)] = raw_t[slot, tap, :MAIN, :MAIN]
                at = 2 * MAIN + f * REST
                wt[slot, at : at + REST, columns(g)] = raw_t[slot, tap, MAIN:, :MAIN]
            rests = jnp.concatenate([raw_t[slot, f - g + 1, :, MAIN:] for g in range(FRAMES)], axis=1)
            wt[slot, f * MAIN : (f + 1) * MAIN, 2 * MAIN :] = rests[:MAIN]
            at = 2 * MAIN + f * REST
            wt[slot, at : at + REST, 2 * MAIN :] = rests[MAIN:]

    half = C // 2
    number = lax.broadcasted_iota(jnp.int32, (8, half), 1).astype(F32)
    which = lax.broadcasted_iota(jnp.int32, (8, half), 0)
    t = jnp.where(which == 0, timesteps[0], timesteps[1]).astype(F32)
    angle = t * jnp.exp(-math.log(10000.0) * number / half)
    emb = jnp.concatenate([jnp.cos(angle), jnp.sin(angle)], axis=1)
    bias = [
        jnp.dot(emb, raw_b[slot], preferred_element_type=F32, precision=lax.Precision.HIGHEST) for slot in range(2)
    ]

    def twice(value):
        return jnp.concatenate([value, value], axis=1)

    gain_main = [gains[slot : slot + 1, :MAIN] for slot in range(2)]
    gain_rest = [twice(gains[slot : slot + 1, MAIN:]) for slot in range(2)]
    two = jnp.full((1, 128), bounds[segment + 1] - bounds[segment], jnp.int32) > 1
    two_main = jnp.concatenate([two, two], axis=1)
    low = lanes((PIX, 128)) < REST

    def first_of(pair):
        return pair[:, :MAIN].astype(F32)

    def second_of(pair):
        return pair[:, MAIN : 2 * MAIN].astype(F32)

    def rests_of(pair):
        return pair[:, 2 * MAIN :].astype(F32)

    for step in range(STEPS):
        bias_main = [bias[slot][step : step + 1, :MAIN] for slot in range(2)]
        bias_rest = [twice(bias[slot][step : step + 1, MAIN:]) for slot in range(2)]
        far, own, near = (arrived.at[step, at] for at in range(3))

        def keep(at, main_a, main_b, rest):
            hidden[at] = jnp.concatenate([main_a, main_b, rest], axis=1).astype(BF16)
            norm_pair(hidden[at], gain_main[1], gain_rest[1], hm, hr, 2 * at, 2 * at + 1, at)

        for part in parts:
            own_copy(step, part).wait_recv()
            inner_copy(step, part).start()

            @pl.when(has_across)
            def _(step=step, part=part):
                across_copy(step, part).start()

            begin, size = PARTS[part]
            spot = slice(begin, begin + size)
            norm_pair(own[spot], gain_main[0], gain_rest[0], xm, xr, 2, 3, 1, spot)
        for tile in range(4):
            zf[:, columns(tile)] = after_part(xm, 2, xr[1], wm.at[0], w_own.at[0], tile)

        for part in parts:
            inner_copy(step, part).wait_recv()
        norm_pair(near[...], gain_main[0], gain_rest[0], xm, xr, 5, 4, 2)
        rests = jnp.concatenate([xr[1], xr[2]], axis=1)
        centre = (second_of(own), second_of(near), jnp.where(low, roll_rest(rests_of(own)), rests_of(near)))
        results = finish(
            lambda tile: both_parts(xm, 2, rests, wm.at[0], w_near, tile), centre, wt.at[0], bias_main[0], bias_rest[0]
        )
        keep(1, *results)
        for tile in range(4):
            zh[:, columns(tile)] = after_part(hm, 2, hr[1], wm.at[1], w_own.at[1], tile)

        @pl.when(has_across)
        def _(step=step):
            for part in parts:
                across_copy(step, part).wait_recv()

        norm_pair(far[...], gain_main[0], gain_rest[0], xm, xr, 1, 0, 0)
        centre = (first_of(far), first_of(own), jnp.where(low, rests_of(far), roll_rest(rests_of(own))))
        main_a, main_b, rest = finish(
            lambda tile: zf[:, columns(tile)] + before_part(xm, 0, xr[0], wm.at[0], w_far, tile),
            centre, wt.at[0], bias_main[0], bias_rest[0],
        )
        keep(0, jnp.where(has_across, main_a, 0.0), main_b, jnp.where(low, jnp.where(has_across, rest, 0.0), rest))
        centre = (
            second_of(hidden.at[0]),
            first_of(hidden.at[1]),
            roll_rest(jnp.where(low, rests_of(hidden.at[1]), rests_of(hidden.at[0]))),
        )
        main_a, main_b, rest = finish(
            lambda tile: zh[:, columns(tile)] + before_part(hm, 0, hr[0], wm.at[1], w_hid, tile),
            centre, wt.at[1], bias_main[1], bias_rest[1],
        )
        main_a = jnp.where(two_main, main_a, centre[0])
        main_b = jnp.where(two_main, main_b, centre[1])
        rest = jnp.where(two, rest, centre[2])
        if step + 1 < STEPS:
            packed[step + 1] = jnp.concatenate([main_a, main_b, rest], axis=1).astype(BF16)
            for part in parts:
                own_copy(step + 1, part).start()
        else:
            for row, main in enumerate((main_a, main_b)):
                for f in range(FRAMES):
                    spot = slice(f * W, (f + 1) * W)
                    ends = rest[spot, row * REST : (row + 1) * REST]
                    out[f, core if row == 0 else 1 - core] = jnp.concatenate([main[spot], ends], axis=1).astype(BF16)

    for step in range(STEPS):
        for part in parts:
            own_copy(step, part).wait_send()
            inner_copy(step, part).wait_send()

        @pl.when(has_across)
        def _(step=step):
            for part in parts:
                across_copy(step, part).wait_send()


def body(state, bounds, timesteps, gains, spatial_weight, temporal_weight, time_weight):
    vmem = pl.BlockSpec(memory_space=pltpu.VMEM)
    smem = pl.BlockSpec(memory_space=pltpu.SMEM)
    hbm = pl.BlockSpec(memory_space=pl.ANY)
    out = pl.pallas_call(
        kernel,
        out_shape=jax.ShapeDtypeStruct((FRAMES, 2, W, C), BF16),
        in_specs=[vmem, smem, smem, vmem, hbm, hbm, hbm],
        out_specs=vmem,
        scratch_shapes=[
            pltpu.VMEM((2, 9, C, C), BF16),
            pltpu.VMEM((2, 3, C, C), BF16),
            pltpu.VMEM((2, C, C), F32),
            pltpu.VMEM((2, 3 * MAIN, NOUT), BF16),
            pltpu.VMEM((2, 4 * REST, NOUT), BF16),
            pltpu.VMEM((2, 2, 2 * REST, NOUT), BF16),
            pltpu.VMEM((2, 2 * REST, NOUT), BF16),
            pltpu.VMEM((2, 2 * REST, NOUT), BF16),
            pltpu.VMEM((2, PACK, PACK), BF16),
            pltpu.VMEM((STEPS, PIX, PACK), BF16),
            pltpu.VMEM((STEPS, 3, PIX, PACK), BF16),
            pltpu.VMEM((2, PIX, PACK), BF16),
            pltpu.VMEM((6, PIX, MAIN), BF16),
            pltpu.VMEM((3, PIX, 128), BF16),
            pltpu.VMEM((4, PIX, MAIN), BF16),
            pltpu.VMEM((2, PIX, 128), BF16),
            pltpu.VMEM((2 * PIX, NOUT), F32),
            pltpu.VMEM((2 * PIX, NOUT), F32),
            pltpu.SemaphoreType.DMA((2, 3)),
            pltpu.SemaphoreType.DMA((STEPS, 3, len(PARTS))),
            pltpu.SemaphoreType.DMA((STEPS, 3, len(PARTS))),
        ],
        compiler_params=pltpu.CompilerParams(
            collective_id=1, has_side_effects=True, vmem_limit_bytes=56 << 20
        ),
        cost_estimate=pl.CostEstimate(flops=4 << 30, bytes_accessed=6 << 20, transcendentals=1 << 20),
        name="cycle",
    )(
        state.reshape(FRAMES, 2, W, C),
        bounds,
        timesteps,
        gains.reshape(2, C),
        spatial_weight.reshape(2, 9, C, C),
        temporal_weight.reshape(2, 3, C, C),
        time_weight.reshape(2, C, C),
    )
    return out.reshape(1, FRAMES, 2, W * C)


def solution(mesh):
    placed = (
        P("segment", None, "rows", None),
        P(),
        P(),
        P("segment", None, None),
        P("segment", None, None, None, None, None),
        P("segment", None, None, None, None),
        P("segment", None, None, None),
    )
    return jax.shard_map(
        body,
        mesh=mesh,
        in_specs=placed,
        out_specs=P("segment", None, "rows", None),
        check_vma=False,
    )
```

time: 40.6 us -> 34.7 us (0.85)
  Pallas kernels: 36.4 us -> 30.8 us
    pallas_call x1, Pallas kernels: 36.4 us -> 30.8 us  [body(): pl.pallas_call(kernel, out_shape=jax.ShapeDtypeStruct((FRAMES, 2, W, C),...]
where the time goes in v2:
time: 34.7 us; the launch traced here: 34.5 us
  Pallas kernels  30.8 us (89%)
  local copies, waits for them, and re-layouts  3.72 us (11%)
    pallas_call x1, Pallas kernels, body(): pl.pallas_call(kernel, out_shape=jax.ShapeDtypeStruct((FRAMES, 2, W, C),...  30.8 us
    reshape x1, local copies, waits for them, and re-layouts, body(): return out.reshape(1, FRAMES, 2, W * C)  1.89 us
    reshape x1, local copies, waits for them, and re-layouts, body(): state.reshape(FRAMES, 2, W, C)  1.83 us

profile of v2, /device:TPU:103, one launch (start us, length us, event | category | flops | bytes accessed | tf_op | source)
XLA Modules:
  0.0 34.5 jit_solution(11781885454937235212)
XLA Ops:
  0.0 1.8 %reshape.18.state = bf16[2,2,72,320]{3,2,1,0:T(8,128)(2,1)} reshape(bf16[1,2,2,23040]{3,2,1,0:T(2,128)(2,1)} %param.7) | data formatting | bytes 368640 | tf_op jit(solution)/shard_map/reshape | solution.py:388
  1.8 30.8 %cycle.1 = bf16[2,2,72,320]{3,2,1,0:T(8,128)(2,1)} custom-call(bf16[2,2,72,320]{3,2,1,0:T(8,128)(2,1)} %reshape.18.state, s32[5]{0:T(128)} %bounds.1, s32[2]{0:T(128)} %timesteps.1, f32[2,320]{1,0:T(2,128)} %bitcast.9, bf16[2,9,320,320]{3,2,1,0:T(8,128)(2,1)} %bitcast.6, bf16[2,3,320,320]{3,2,1,0:T(8,128)(2,1)} %bitcast.7, f32[2,320,320]{2,1,0:T(8,128)} %bitcast.8), custom_call_target="tpu_custom_call" | custom-call | flops 4294967296 | bytes 6291456 | tf_op jit(solution)/shard_map/cycle/pallas_call | solution.py:354
  32.6 1.9 %reshape.23 = bf16[1,2,2,23040]{3,2,1,0:T(2,128)(2,1)} reshape(bf16[2,2,72,320]{3,2,1,0:T(8,128)(2,1)} %cycle.1) | data formatting | bytes 368640 | tf_op jit(solution)/shard_map/reshape | solution.py:396

commit v3 on v2

--- a/solution.py
+++ b/solution.py
@@ -17,6 +17,7 @@
 REST = C - MAIN
 PIX = FRAMES * W
 PACK = 2 * MAIN + 2 * REST
+TILES = 2 * C // 128
 NOUT = 4 * MAIN
 PARTS = ((0, 48), (48, 48), (96, 48))
 NEAR = ((0, 1, None, 2), (None, 0, 2, 1))
@@ -139,7 +140,7 @@
 def kernel(
     state, bounds, timesteps, gains, spatial, temporal, time_weight,
     out,
-    raw_s, raw_t, raw_b, wm, w_near, w_own, w_far, w_hid, wt, packed, arrived, hidden, xm, xr, hm, hr, zf, zh,
+    raw_x, strip, pixels, raw_s, raw_t, raw_b, wm, w_near, w_own, w_far, w_hid, wt, packed, arrived, hidden, xm, xr, hm, hr, zf, zh,
     load_sem, send_sem, recv_sem,
 ):
     segment = lax.axis_index("segment")
@@ -168,13 +169,26 @@
     def _():
         pl.semaphore_signal(barrier, inc=1, device_id=(segment, across), device_id_type=MESH)
 
-    for load in loads[0] + loads[1]:
+    state_load = pltpu.make_async_copy(state.at[0], raw_x, load_sem.at[2, 0])
+    for load in (state_load, *loads[0], *loads[1]):
         load.start()
 
-    rows = [[state[f, row].astype(F32) for f in range(FRAMES)] for row in (core, 1 - core)]
-    main = [jnp.concatenate([x[:, :MAIN] for x in row], axis=0) for row in rows]
-    rest = [jnp.concatenate([x[:, MAIN:] for x in row], axis=0) for row in rows]
-    packed[0] = jnp.concatenate(main + rest, axis=1).astype(BF16)
+    state_load.wait()
+    low_half = lanes((W // 2, 128)) < REST
+    for f in range(FRAMES):
+        for pair in range(W // 2):
+            for k in range(TILES):
+                begin = 2 * C * pair + 128 * k
+                strip[f, k, 2 * pair : 2 * pair + 2] = raw_x[f, :, begin : begin + 128].astype(F32)
+        for row, at in ((0, core), (1, 1 - core)):
+            own = [strip[f, k, pl.ds(row, W // 2, stride=2)] for k in range(TILES)]
+            swapped = [None, None] + [roll_rest(tile) for tile in own[2:]]
+            odd = [jnp.where(low_half, swapped[2 + k], swapped[min(3 + k, 4)]) for k in range(3)]
+            for k in range(3):
+                pixels[at, k, pl.ds(f * W, W // 2, stride=2)] = own[k]
+                pixels[at, k, pl.ds(f * W + 1, W // 2, stride=2)] = odd[k]
+    rest = jnp.where(lanes((PIX, 128)) < REST, pixels[0, 2], roll_rest(pixels[1, 2]))
+    packed[0] = jnp.concatenate([pixels[at, k] for at in range(2) for k in range(2)] + [rest], axis=1).astype(BF16)
 
     pl.semaphore_wait(barrier, 2 + has_across.astype(jnp.int32))
 
@@ -330,11 +344,22 @@
             for part in parts:
                 own_copy(step + 1, part).start()
         else:
-            for row, main in enumerate((main_a, main_b)):
-                for f in range(FRAMES):
-                    spot = slice(f * W, (f + 1) * W)
-                    ends = rest[spot, row * REST : (row + 1) * REST]
-                    out[f, core if row == 0 else 1 - core] = jnp.concatenate([main[spot], ends], axis=1).astype(BF16)
+            for at, (main, ends) in enumerate(((main_a, rest), (main_b, roll_rest(rest)))):
+                pixels[at, 0], pixels[at, 1], pixels[at, 2] = main[:, :128], main[:, 128:], ends
+            for f in range(FRAMES):
+                for row, at in ((0, core), (1, 1 - core)):
+                    even, odd = (
+                        [pixels[at, k, pl.ds(f * W + one, W // 2, stride=2)] for k in range(3)] for one in range(2)
+                    )
+                    odd = [roll_rest(tile) for tile in odd]
+                    own = [even[0], even[1]]
+                    own += [jnp.where(low_half, one, two) for one, two in ((even[2], odd[0]), odd[:2], odd[1:])]
+                    for k in range(TILES):
+                        strip[f, k, pl.ds(row, W // 2, stride=2)] = own[k]
+                for pair in range(W // 2):
+                    for k in range(TILES):
+                        begin = 2 * C * pair + 128 * k
+                        out[0, f, :, begin : begin + 128] = strip[f, k, 2 * pair : 2 * pair + 2].astype(BF16)
 
     for step in range(STEPS):
         for part in parts:
@@ -351,12 +376,15 @@
     vmem = pl.BlockSpec(memory_space=pltpu.VMEM)
     smem = pl.BlockSpec(memory_space=pltpu.SMEM)
     hbm = pl.BlockSpec(memory_space=pl.ANY)
-    out = pl.pallas_call(
+    return pl.pallas_call(
         kernel,
-        out_shape=jax.ShapeDtypeStruct((FRAMES, 2, W, C), BF16),
-        in_specs=[vmem, smem, smem, vmem, hbm, hbm, hbm],
+        out_shape=jax.ShapeDtypeStruct((1, FRAMES, 2, W * C), BF16),
+        in_specs=[hbm, smem, smem, vmem, hbm, hbm, hbm],
         out_specs=vmem,
         scratch_shapes=[
+            pltpu.VMEM((FRAMES, 2, W * C), BF16),
+            pltpu.VMEM((FRAMES, TILES, W, 128), F32),
+            pltpu.VMEM((2, 3, PIX, 128), F32),
             pltpu.VMEM((2, 9, C, C), BF16),
             pltpu.VMEM((2, 3, C, C), BF16),
             pltpu.VMEM((2, C, C), F32),
@@ -375,7 +403,7 @@
             pltpu.VMEM((2, PIX, 128), BF16),
             pltpu.VMEM((2 * PIX, NOUT), F32),
             pltpu.VMEM((2 * PIX, NOUT), F32),
-            pltpu.SemaphoreType.DMA((2, 3)),
+            pltpu.SemaphoreType.DMA((3, 3)),
             pltpu.SemaphoreType.DMA((STEPS, 3, len(PARTS))),
             pltpu.SemaphoreType.DMA((STEPS, 3, len(PARTS))),
         ],
@@ -385,7 +413,7 @@
         cost_estimate=pl.CostEstimate(flops=4 << 30, bytes_accessed=6 << 20, transcendentals=1 << 20),
         name="cycle",
     )(
-        state.reshape(FRAMES, 2, W, C),
+        state,
         bounds,
         timesteps,
         gains.reshape(2, C),
@@ -393,7 +421,6 @@
         temporal_weight.reshape(2, 3, C, C),
         time_weight.reshape(2, C, C),
     )
-    return out.reshape(1, FRAMES, 2, W * C)
 
 
 def solution(mesh):

time: 34.7 us -> 32.5 us (0.937)
  local copies, waits for them, and re-layouts: 3.72 us -> 1.72 us
    reshape x2 -> x0, local copies, waits for them, and re-layouts: 3.72 us -> none  [the longest x1 1.89 us: body(): return out.reshape(1, FRAMES, 2, W * C)]
    unnamed x0 -> x1, local copies, waits for them, and re-layouts: none -> 1.72 us
where the time goes in v3:
time: 32.5 us; the launch traced here: 32.4 us
  Pallas kernels  30.7 us (94%)
  local copies, waits for them, and re-layouts  1.72 us (5%)
    pallas_call x1, Pallas kernels, body(): pl.pallas_call(kernel, out_shape=jax.ShapeDtypeStruct((1, FRAMES, 2, W *...  30.7 us
    unnamed x1, local copies, waits for them, and re-layouts  1.72 us

profile of v3, /device:TPU:103, one launch (start us, length us, event | category | flops | bytes accessed | tf_op | source)
XLA Modules:
  0.0 32.4 jit_solution(6118477321438168801)
XLA Ops:
  0.0 30.7 %cycle.1 = bf16[1,2,2,23040]{3,2,1,0:T(2,128)(2,1)} custom-call(bf16[1,2,2,23040]{3,2,1,0:T(2,128)(2,1)} %state.1, s32[5]{0:T(128)} %bounds.1, s32[2]{0:T(128)} %timesteps.1, f32[2,320]{1,0:T(2,128)} %bitcast.7, bf16[2,9,320,320]{3,2,1,0:T(8,128)(2,1)} %bitcast.4, bf16[2,3,320,320]{3,2,1,0:T(8,128)(2,1)} %bitcast.5, f32[2,320,320]{2,1,0:T(8,128)} %bitcast.6), custom_call_target="tpu_custom_call" | custom-call | flops 4294967296 | bytes 6291456 | tf_op jit(solution)/shard_map/cycle/pallas_call | solution.py:379
  30.7 1.7 %copy.9 = bf16[1,2,2,23040]{3,2,1,0:T(2,128)(2,1)} copy(bf16[1,2,2,23040]{3,2,1,0:T(2,128)(2,1)} %cycle.1) | data formatting | bytes 368640

commit v4 on v3

--- a/solution.py
+++ b/solution.py
@@ -55,6 +55,18 @@
     xm[first, spot] = (main_a * scale_a * gain_main).astype(BF16)
     xm[second, spot] = (main_b * scale_b * gain_main).astype(BF16)
     xr[at, spot] = (rest * jnp.where(low, scale_a, scale_b) * gain_rest).astype(BF16)
+
+
+def first_of(pair):
+    return pair[:, :MAIN].astype(F32)
+
+
+def second_of(pair):
+    return pair[:, MAIN : 2 * MAIN].astype(F32)
+
+
+def rests_of(pair):
+    return pair[:, 2 * MAIN :].astype(F32)
 
 
 def dot(left, right):
@@ -271,15 +283,6 @@
     two_main = jnp.concatenate([two, two], axis=1)
     low = lanes((PIX, 128)) < REST
 
-    def first_of(pair):
-        return pair[:, :MAIN].astype(F32)
-
-    def second_of(pair):
-        return pair[:, MAIN : 2 * MAIN].astype(F32)
-
-    def rests_of(pair):
-        return pair[:, 2 * MAIN :].astype(F32)
-
     for step in range(STEPS):
         bias_main = [bias[slot][step : step + 1, :MAIN] for slot in range(2)]
         bias_rest = [twice(bias[slot][step : step + 1, MAIN:]) for slot in range(2)]
@@ -344,22 +347,7 @@
             for part in parts:
                 own_copy(step + 1, part).start()
         else:
-            for at, (main, ends) in enumerate(((main_a, rest), (main_b, roll_rest(rest)))):
-                pixels[at, 0], pixels[at, 1], pixels[at, 2] = main[:, :128], main[:, 128:], ends
-            for f in range(FRAMES):
-                for row, at in ((0, core), (1, 1 - core)):
-                    even, odd = (
-                        [pixels[at, k, pl.ds(f * W + one, W // 2, stride=2)] for k in range(3)] for one in range(2)
-                    )
-                    odd = [roll_rest(tile) for tile in odd]
-                    own = [even[0], even[1]]
-                    own += [jnp.where(low_half, one, two) for one, two in ((even[2], odd[0]), odd[:2], odd[1:])]
-                    for k in range(TILES):
-                        strip[f, k, pl.ds(row, W // 2, stride=2)] = own[k]
-                for pair in range(W // 2):
-                    for k in range(TILES):
-                        begin = 2 * C * pair + 128 * k
-                        out[0, f, :, begin : begin + 128] = strip[f, k, 2 * pair : 2 * pair + 2].astype(BF16)
+            out[...] = jnp.concatenate([main_a, main_b, rest], axis=1).astype(BF16)
 
     for step in range(STEPS):
         for part in parts:
@@ -372,13 +360,35 @@
                 across_copy(step, part).wait_send()
 
 
+def unpack(pair, out, strip, pixels):
+    core = lax.rem(lax.axis_index("rows"), 2)
+    low_half = lanes((W // 2, 128)) < REST
+    rest = rests_of(pair)
+    for at, (main, ends) in enumerate(((first_of(pair), rest), (second_of(pair), roll_rest(rest)))):
+        pixels[at, 0], pixels[at, 1], pixels[at, 2] = main[:, :128], main[:, 128:], ends
+    for f in range(FRAMES):
+        for row, at in ((0, core), (1, 1 - core)):
+            even, odd = (
+                [pixels[at, k, pl.ds(f * W + one, W // 2, stride=2)] for k in range(3)] for one in range(2)
+            )
+            odd = [roll_rest(tile) for tile in odd]
+            own = [even[0], even[1]]
+            own += [jnp.where(low_half, one, two) for one, two in ((even[2], odd[0]), odd[:2], odd[1:])]
+            for k in range(TILES):
+                strip[f, k, pl.ds(row, W // 2, stride=2)] = own[k]
+        for pair in range(W // 2):
+            for k in range(TILES):
+                begin = 2 * C * pair + 128 * k
+                out[0, f, :, begin : begin + 128] = strip[f, k, 2 * pair : 2 * pair + 2].astype(BF16)
+
+
 def body(state, bounds, timesteps, gains, spatial_weight, temporal_weight, time_weight):
     vmem = pl.BlockSpec(memory_space=pltpu.VMEM)
     smem = pl.BlockSpec(memory_space=pltpu.SMEM)
     hbm = pl.BlockSpec(memory_space=pl.ANY)
-    return pl.pallas_call(
+    pair = pl.pallas_call(
         kernel,
-        out_shape=jax.ShapeDtypeStruct((1, FRAMES, 2, W * C), BF16),
+        out_shape=pltpu.VMEM((PIX, PACK), BF16),
         in_specs=[hbm, smem, smem, vmem, hbm, hbm, hbm],
         out_specs=vmem,
         scratch_shapes=[
@@ -421,6 +431,15 @@
         temporal_weight.reshape(2, 3, C, C),
         time_weight.reshape(2, C, C),
     )
+    return pl.pallas_call(
+        unpack,
+        out_shape=jax.ShapeDtypeStruct((1, FRAMES, 2, W * C), BF16),
+        in_specs=[vmem],
+        out_specs=vmem,
+        scratch_shapes=[pltpu.VMEM((FRAMES, TILES, W, 128), F32), pltpu.VMEM((2, 3, PIX, 128), F32)],
+        compiler_params=pltpu.CompilerParams(vmem_limit_bytes=16 << 20),
+        name="unpack",
+    )(pair)
 
 
 def solution(mesh):

time: 32.5 us -> 30.8 us (0.948)
  local copies, waits for them, and re-layouts: 1.72 us -> 0 us
    unnamed x1 -> x0, local copies, waits for them, and re-layouts: 1.72 us -> none
    pallas_call x1 -> x2, Pallas kernels: 30.7 us -> 30.7 us  [the longest x1 29.8 us: body(): pl.pallas_call(kernel, out_shape=pltpu.VMEM((PIX, PACK), BF16), in_specs=...]
where the time goes in v4:
time: 30.8 us; the launch traced here: 30.7 us
  Pallas kernels  30.7 us (100%)
    pallas_call x1, Pallas kernels, body(): pl.pallas_call(kernel, out_shape=pltpu.VMEM((PIX, PACK), BF16), in_specs=...  29.8 us
    pallas_call x1, Pallas kernels, body(): pl.pallas_call(unpack, out_shape=jax.ShapeDtypeStruct((1, FRAMES, 2, W *...  0.92 us

profile of v4, /device:TPU:103, one launch (start us, length us, event | category | flops | bytes accessed | tf_op | source)
XLA Modules:
  0.0 30.7 jit_solution(13880674155103351605)
XLA Ops:
  0.0 29.8 %cycle.1.pair = bf16[144,640]{1,0:T(8,128)(2,1)S(1)} custom-call(bf16[1,2,2,23040]{3,2,1,0:T(2,128)(2,1)} %state.1, s32[5]{0:T(128)} %bounds.1, s32[2]{0:T(128)} %timesteps.1, f32[2,320]{1,0:T(2,128)} %bitcast.7, bf16[2,9,320,320]{3,2,1,0:T(8,128)(2,1)} %bitcast.4, bf16[2,3,320,320]{3,2,1,0:T(8,128)(2,1)} %bitcast.5, f32[2,320,320]{2,1,0:T(8,128)} %bitcast.6), custom_call_target="tpu_custom_call" | custom-call | flops 4294967296 | bytes 6291456 | tf_op jit(solution)/shard_map/cycle/pallas_call | solution.py:389
  29.8 0.9 %unpack.1 = bf16[1,2,2,23040]{3,2,1,0:T(2,128)(2,1)} custom-call(bf16[144,640]{1,0:T(8,128)(2,1)S(1)} %cycle.1.pair), custom_call_target="tpu_custom_call" | custom-call | tf_op jit(solution)/shard_map/unpack/pallas_call | solution.py:434

commit v5 on v4

--- a/solution.py
+++ b/solution.py
@@ -18,8 +18,9 @@
 PIX = FRAMES * W
 PACK = 2 * MAIN + 2 * REST
 TILES = 2 * C // 128
-NOUT = 4 * MAIN
-PARTS = ((0, 48), (48, 48), (96, 48))
+NOUT = 3 * MAIN
+NENDS = 3 * 128
+PARTS = ((0, 32), (32, 32), (64, 32), (96, 32), (128, 16))
 NEAR = ((0, 1, None, 2), (None, 0, 2, 1))
 AFTER = ((2, None), (1, 2))
 BEFORE = ((0, 1), (None, 0))
@@ -77,82 +78,78 @@
     return slice(tile * MAIN, (tile + 1) * MAIN)
 
 
-def before_part(xm, row, rest, wm, wr, tile):
+def before_part(xm, row, rest, wm, wr, we, we_rest, tile, out_row):
     cols = columns(tile)
-    one = dot(jnp.concatenate([xm[row], xm[row + 1]], axis=1), wm[: 2 * MAIN, cols]) + dot(rest, wr[0, :, cols])
-    two = dot(xm[row + 1], wm[:MAIN, cols]) + dot(rest, wr[1, :, cols])
+    both = jnp.concatenate([xm[row], xm[row + 1]], axis=1)
+    if tile == 3:
+        return dot(both, we[: 2 * MAIN]) + dot(rest, we_rest[...])
+    if out_row == 0:
+        return dot(both, wm[: 2 * MAIN, cols]) + dot(rest, wr[0, :, cols])
+    return dot(xm[row + 1], wm[:MAIN, cols]) + dot(rest, wr[1, :, cols])
+
+
+def after_part(xm, row, rest, wm, wr, we, we_rest, tile):
+    cols = columns(tile)
+    both = jnp.concatenate([xm[row], xm[row + 1]], axis=1)
+    if tile == 3:
+        return dot(both, we[2 * MAIN :]) + dot(rest, we_rest[...])
+    one = dot(xm[row], wm[2 * MAIN :, cols]) + dot(rest, wr[0, :, cols])
+    two = dot(both, wm[MAIN:, cols]) + dot(rest, wr[1, :, cols])
     return jnp.concatenate([one, two], axis=0)
 
 
-def after_part(xm, row, rest, wm, wr, tile):
+def both_parts(xm, row, rest, wm, wr, we, we_rest, tile):
     cols = columns(tile)
-    one = dot(xm[row], wm[2 * MAIN :, cols]) + dot(rest, wr[0, :, cols])
-    two = dot(jnp.concatenate([xm[row], xm[row + 1]], axis=1), wm[MAIN:, cols]) + dot(rest, wr[1, :, cols])
-    return jnp.concatenate([one, two], axis=0)
-
-
-def both_parts(xm, row, rest, wm, wr, tile):
-    cols = columns(tile)
+    if tile == 3:
+        return dot(jnp.concatenate([xm[row + at] for at in range(4)], axis=1), we[...]) + dot(rest, we_rest[...])
     left = jnp.concatenate([xm[row + dy : row + dy + 2].reshape(2 * PIX, MAIN) for dy in range(3)], axis=1)
     rests = jnp.concatenate([dot(rest, wr[0, :, cols]), dot(rest, wr[1, :, cols])], axis=0)
     return dot(left, wm[:, cols]) + rests
 
 
 def finish(product, centre, wt, bias_main, bias_rest):
-    spot = lax.rem(lax.broadcasted_iota(jnp.int32, (2 * PIX, 1), 0), W)
-    first, last = spot == 0, spot == W - 1
+    wt_main, wt_rest, wt_ends = wt
 
     def from_before(value):
-        return jnp.where(first, 0.0, pltpu.roll(value, 1, 0))
+        spot = lax.rem(lax.broadcasted_iota(jnp.int32, (value.shape[0], 1), 0), W)
+        return jnp.where(spot == 0, 0.0, pltpu.roll(value, 1, 0))
 
     def from_after(value):
-        return jnp.where(last, 0.0, pltpu.roll(value, value.shape[0] - 1, 0))
-
-    a_main = from_before(product(0)) + product(1) + from_after(product(2)) + bias_main
-    z = product(3)
-    sides = from_before(z[:, :128]) + from_after(z[:, 128:])
-    middle = z[:, :128]
-    low = lanes((PIX, 128)) < REST
-    a_rest = jnp.where(
-        low,
-        sides[:PIX] + roll_rest(middle[:PIX]),
-        roll_rest(sides[PIX:]) + middle[PIX:],
-    ) + bias_rest
+        spot = lax.rem(lax.broadcasted_iota(jnp.int32, (value.shape[0], 1), 0), W)
+        return jnp.where(spot == W - 1, 0.0, pltpu.roll(value, value.shape[0] - 1, 0))
 
     def silu(value):
         return value * (0.5 * jnp.tanh(0.5 * value) + 0.5)
 
-    u_main = silu(a_main)
+    z = product(3, None)
+    a_rest = from_before(z[:, :128]) + z[:, 128:256] + from_after(z[:, 256:]) + bias_rest
     u_rest = silu(a_rest)
-    low = lanes((W, 128)) < REST
-
-    def transposed(first_half, second_half):
-        return (
-            jnp.where(low, first_half, roll_rest(second_half)),
-            jnp.where(low, roll_rest(first_half), second_half),
-        )
-
-    rest_a, rest_b = transposed(u_rest[:W], u_rest[W:])
-    mixed = jnp.concatenate(
-        [
-            jnp.concatenate([u_main[:W], u_main[PIX : PIX + W]], axis=0),
-            jnp.concatenate([u_main[W:PIX], u_main[PIX + W :]], axis=0),
-            jnp.concatenate([rest_a, rest_b], axis=0),
-        ],
-        axis=1,
-    ).astype(BF16)
-    v = dot(mixed, wt[...])
-    v_a = jnp.concatenate([v[:W, :MAIN], v[:W, MAIN : 2 * MAIN]], axis=0)
-    v_b = jnp.concatenate([v[W:, :MAIN], v[W:, MAIN : 2 * MAIN]], axis=0)
-    v_rest = jnp.concatenate(transposed(v[:W, 2 * MAIN :], v[W:, 2 * MAIN :]), axis=0)
+    a_main, lines = [], []
+    for row in range(2):
+        taps = [product(tile, row) for tile in range(3)]
+        a_main.append(from_before(taps[0]) + taps[1] + from_after(taps[2]) + bias_main)
+        u_main = silu(a_main[row])
+        lines.append([u_main[:W], u_main[W:]])
+    mixed = jnp.concatenate([jnp.concatenate([lines[row][f] for row in range(2)], axis=0) for f in range(FRAMES)], axis=1)
+    mixed = mixed.astype(BF16)
+    ends = jnp.concatenate([u_rest[:W], u_rest[W:]], axis=1).astype(BF16)
+    wide = jnp.concatenate([lines[row][f] for row in range(2) for f in range(FRAMES)], axis=1).astype(BF16)
+    v_rest = dot(wide, wt_ends[: 4 * MAIN]) + dot(ends, wt_ends[4 * MAIN :])
+    v = dot(mixed, wt_main[...])
+    v_rows = []
+    for row in range(2):
+        own = v[row * W : (row + 1) * W] + dot(ends, wt_rest[row])
+        v_rows.append(jnp.concatenate([own[:, :MAIN], own[:, MAIN:]], axis=0))
+    v_rest = jnp.concatenate([v_rest[:, :128], v_rest[:, 128:]], axis=0)
     h_a, h_b, h_rest = centre
-    return h_a + a_main[:PIX] + v_a, h_b + a_main[PIX:] + v_b, h_rest + a_rest + v_rest
+    return h_a + a_main[0] + v_rows[0], h_b + a_main[1] + v_rows[1], h_rest + a_rest + v_rest
 
 
 def kernel(
     state, bounds, timesteps, gains, spatial, temporal, time_weight,
     out,
-    raw_x, strip, pixels, raw_s, raw_t, raw_b, wm, w_near, w_own, w_far, w_hid, wt, packed, arrived, hidden, xm, xr, hm, hr, zf, zh,
+    raw_x, strip, pixels, raw_s, raw_t, raw_b, wm, w_near, w_own, w_far, w_hid, we, e_near, e_own, e_far, e_hid, wt_main, wt_rest, wt_ends,
+    packed, arrived, hidden, xm, xr, hm, hr, zf, zh, zfe, zhe,
     load_sem, send_sem, recv_sem,
 ):
     segment = lax.axis_index("segment")
@@ -230,6 +227,7 @@
             arrived[step, 0] = jnp.zeros((PIX, PACK), BF16)
 
     none = jnp.zeros((REST, NOUT), BF16)
+    wt = [(wt_main.at[slot], wt_rest.at[slot], wt_ends.at[slot]) for slot in range(2)]
     for slot in range(2):
         for load in loads[slot]:
             load.wait()
@@ -237,32 +235,47 @@
             taps = [3 * (dy + core * (2 - 2 * dy)) + dx for dx in range(3)]
             for dx in range(3):
                 wm[slot, dy * MAIN : (dy + 1) * MAIN, columns(dx)] = raw_s[slot, taps[dx], :MAIN, :MAIN]
-            rests = [raw_s[slot, tap, :, MAIN:] for tap in taps]
-            rests = jnp.concatenate(rests + [jnp.zeros_like(rests[0])], axis=1)
-            wm[slot, dy * MAIN : (dy + 1) * MAIN, columns(3)] = rests[:MAIN]
-            tail = jnp.concatenate([raw_s[slot, tap, MAIN:, :MAIN] for tap in taps] + [rests[MAIN:]], axis=1)
+            tail = jnp.concatenate([raw_s[slot, tap, MAIN:, :MAIN] for tap in taps], axis=1)
             if slot == 0:
-                places = ((w_near, NEAR), (w_own, AFTER), (w_far, BEFORE_REVERSED))
+                places = ((w_near, NEAR), (w_own.at[slot], AFTER), (w_far, BEFORE_REVERSED))
             else:
-                places = ((w_own, AFTER), (w_hid, BEFORE))
+                places = ((w_own.at[slot], AFTER), (w_hid, BEFORE))
             for ref, order in places:
-                ref = ref.at[slot] if ref is w_own else ref
                 for row in range(2):
                     for at, tap in enumerate(order[row]):
                         if tap == dy:
                             ref[row, at * REST : (at + 1) * REST] = tail
                         elif tap is None and dy == 0:
                             ref[row, at * REST : (at + 1) * REST] = none
+        blank = jnp.zeros((C, REST), BF16)
+
+        def ends_of(i):
+            tap = lambda dy, dx: raw_s[slot, 3 * (dy + core * (2 - 2 * dy)) + dx, :, MAIN:] if 0 <= dy < 3 else blank
+            return jnp.concatenate([tap(i - row, dx) for dx in range(3) for row in range(2)], axis=1)
+
+        ends = [ends_of(i) for i in range(4)]
+        for i in range(4):
+            we[slot, i * MAIN : (i + 1) * MAIN] = ends[i][:MAIN]
+        places = ((e_near, (0, 1, 3, 2)), (e_own.at[slot], (2, 3)), (e_far, (1, 0)))
+        for ref, order in places if slot == 0 else ((e_own.at[slot], (2, 3)), (e_hid, (0, 1))):
+            for at, i in enumerate(order):
+                ref[at * REST : (at + 1) * REST] = ends[i][MAIN:]
+        nil = jnp.zeros((REST, FRAMES * MAIN), BF16)
+        blank = jnp.zeros((C, REST), BF16)
         for f in range(FRAMES):
+            taps = [f - g + 1 for g in range(FRAMES)]
             for g in range(FRAMES):
-                tap = f - g + 1
-                wt[slot, f * MAIN : (f + 1) * MAIN, columns(g)] = raw_t[slot, tap, :MAIN, :MAIN]
-                at = 2 * MAIN + f * REST
-                wt[slot, at : at + REST, columns(g)] = raw_t[slot, tap, MAIN:, :MAIN]
-            rests = jnp.concatenate([raw_t[slot, f - g + 1, :, MAIN:] for g in range(FRAMES)], axis=1)
-            wt[slot, f * MAIN : (f + 1) * MAIN, 2 * MAIN :] = rests[:MAIN]
-            at = 2 * MAIN + f * REST
-            wt[slot, at : at + REST, 2 * MAIN :] = rests[MAIN:]
+                wt_main[slot, f * MAIN : (f + 1) * MAIN, columns(g)] = raw_t[slot, taps[g], :MAIN, :MAIN]
+            tail = jnp.concatenate([raw_t[slot, tap, MAIN:, :MAIN] for tap in taps], axis=1)
+            for row in range(2):
+                for at in range(2):
+                    begin = (2 * f + at) * REST
+                    wt_rest[slot, row, begin : begin + REST] = tail if at == row else nil
+                ends = [raw_t[slot, tap, :, MAIN:] for tap in taps]
+                ends = jnp.concatenate([ends[g] if at == row else blank for g in range(FRAMES) for at in range(2)], axis=1)
+                wt_ends[slot, (2 * row + f) * MAIN : (2 * row + f + 1) * MAIN] = ends[:MAIN]
+                begin = 4 * MAIN + (2 * f + row) * REST
+                wt_ends[slot, begin : begin + REST] = ends[MAIN:]
 
     half = C // 2
     number = lax.broadcasted_iota(jnp.int32, (8, half), 1).astype(F32)
@@ -304,19 +317,33 @@
             spot = slice(begin, begin + size)
             norm_pair(own[spot], gain_main[0], gain_rest[0], xm, xr, 2, 3, 1, spot)
         for tile in range(4):
-            zf[:, columns(tile)] = after_part(xm, 2, xr[1], wm.at[0], w_own.at[0], tile)
+            part = after_part(xm, 2, xr[1], wm.at[0], w_own.at[0], we.at[0], e_own.at[0], tile)
+            if tile == 3:
+                zfe[...] = part
+            else:
+                zf[:, columns(tile)] = part
 
         for part in parts:
             inner_copy(step, part).wait_recv()
         norm_pair(near[...], gain_main[0], gain_rest[0], xm, xr, 5, 4, 2)
         rests = jnp.concatenate([xr[1], xr[2]], axis=1)
-        centre = (second_of(own), second_of(near), jnp.where(low, roll_rest(rests_of(own)), rests_of(near)))
+        own_turned = roll_rest(rests_of(own))
+        centre = (second_of(own), second_of(near), jnp.where(low, own_turned, rests_of(near)))
+        products = [both_parts(xm, 2, rests, wm.at[0], w_near, we.at[0], e_near, tile) for tile in range(4)]
         results = finish(
-            lambda tile: both_parts(xm, 2, rests, wm.at[0], w_near, tile), centre, wt.at[0], bias_main[0], bias_rest[0]
+            lambda tile, row: products[tile] if row is None else products[tile][row * PIX : (row + 1) * PIX],
+            centre, wt[0], bias_main[0], bias_rest[0],
         )
         keep(1, *results)
         for tile in range(4):
-            zh[:, columns(tile)] = after_part(hm, 2, hr[1], wm.at[1], w_own.at[1], tile)
+            part = after_part(hm, 2, hr[1], wm.at[1], w_own.at[1], we.at[1], e_own.at[1], tile)
+            if tile == 3:
+                zhe[...] = part
+            else:
+                zh[:, columns(tile)] = part
+
+        def early(z, ends, tile, row):
+            return ends[...] if row is None else z[row * PIX : (row + 1) * PIX, columns(tile)]
 
         @pl.when(has_across)
         def _(step=step):
@@ -324,10 +351,10 @@
                 across_copy(step, part).wait_recv()
 
         norm_pair(far[...], gain_main[0], gain_rest[0], xm, xr, 1, 0, 0)
-        centre = (first_of(far), first_of(own), jnp.where(low, rests_of(far), roll_rest(rests_of(own))))
+        centre = (first_of(far), first_of(own), jnp.where(low, rests_of(far), own_turned))
         main_a, main_b, rest = finish(
-            lambda tile: zf[:, columns(tile)] + before_part(xm, 0, xr[0], wm.at[0], w_far, tile),
-            centre, wt.at[0], bias_main[0], bias_rest[0],
+            lambda tile, row: early(zf, zfe, tile, row) + before_part(xm, 0, xr[0], wm.at[0], w_far, we.at[0], e_far, tile, row),
+            centre, wt[0], bias_main[0], bias_rest[0],
         )
         keep(0, jnp.where(has_across, main_a, 0.0), main_b, jnp.where(low, jnp.where(has_across, rest, 0.0), rest))
         centre = (
@@ -336,8 +363,8 @@
             roll_rest(jnp.where(low, rests_of(hidden.at[1]), rests_of(hidden.at[0]))),
         )
         main_a, main_b, rest = finish(
-            lambda tile: zh[:, columns(tile)] + before_part(hm, 0, hr[0], wm.at[1], w_hid, tile),
-            centre, wt.at[1], bias_main[1], bias_rest[1],
+            lambda tile, row: early(zh, zhe, tile, row) + before_part(hm, 0, hr[0], wm.at[1], w_hid, we.at[1], e_hid, tile, row),
+            centre, wt[1], bias_main[1], bias_rest[1],
         )
         main_a = jnp.where(two_main, main_a, centre[0])
         main_b = jnp.where(two_main, main_b, centre[1])
@@ -403,7 +430,14 @@
             pltpu.VMEM((2, 2, 2 * REST, NOUT), BF16),
             pltpu.VMEM((2, 2 * REST, NOUT), BF16),
             pltpu.VMEM((2, 2 * REST, NOUT), BF16),
-            pltpu.VMEM((2, PACK, PACK), BF16),
+            pltpu.VMEM((2, 4 * MAIN, NENDS), BF16),
+            pltpu.VMEM((4 * REST, NENDS), BF16),
+            pltpu.VMEM((2, 2 * REST, NENDS), BF16),
+            pltpu.VMEM((2 * REST, NENDS), BF16),
+            pltpu.VMEM((2 * REST, NENDS), BF16),
+            pltpu.VMEM((2, 2 * MAIN, 2 * MAIN), BF16),
+            pltpu.VMEM((2, 2, 4 * REST, 2 * MAIN), BF16),
+            pltpu.VMEM((2, 4 * MAIN + 4 * REST, 4 * REST), BF16),
             pltpu.VMEM((STEPS, PIX, PACK), BF16),
             pltpu.VMEM((STEPS, 3, PIX, PACK), BF16),
             pltpu.VMEM((2, PIX, PACK), BF16),
@@ -413,6 +447,8 @@
             pltpu.VMEM((2, PIX, 128), BF16),
             pltpu.VMEM((2 * PIX, NOUT), F32),
             pltpu.VMEM((2 * PIX, NOUT), F32),
+            pltpu.VMEM((PIX, NENDS), F32),
+            pltpu.VMEM((PIX, NENDS), F32),
             pltpu.SemaphoreType.DMA((3, 3)),
             pltpu.SemaphoreType.DMA((STEPS, 3, len(PARTS))),
             pltpu.SemaphoreType.DMA((STEPS, 3, len(PARTS))),

time: 30.8 us -> 30.1 us (0.977)
  Pallas kernels: 30.7 us -> 30 us
    pallas_call x1, Pallas kernels: 29.8 us -> 29.1 us  [body(): pl.pallas_call(kernel, out_shape=pltpu.VMEM((PIX, PACK), BF16), in_specs=...]
where the time goes in v5:
time: 30.1 us; the launch traced here: 30 us
  Pallas kernels  30 us (100%)
    pallas_call x1, Pallas kernels, body(): pl.pallas_call(kernel, out_shape=pltpu.VMEM((PIX, PACK), BF16), in_specs=...  29.1 us
    pallas_call x1, Pallas kernels, body(): pl.pallas_call(unpack, out_shape=jax.ShapeDtypeStruct((1, FRAMES, 2, W *...  0.92 us

profile of v5, /device:TPU:103, one launch (start us, length us, event | category | flops | bytes accessed | tf_op | source)
XLA Modules:
  0.0 30.0 jit_solution(11358637135520453852)
XLA Ops:
  0.0 29.1 %cycle.1.pair = bf16[144,640]{1,0:T(8,128)(2,1)S(1)} custom-call(bf16[1,2,2,23040]{3,2,1,0:T(2,128)(2,1)} %state.1, s32[5]{0:T(128)} %bounds.1, s32[2]{0:T(128)} %timesteps.1, f32[2,320]{1,0:T(2,128)} %bitcast.7, bf16[2,9,320,320]{3,2,1,0:T(8,128)(2,1)} %bitcast.4, bf16[2,3,320,320]{3,2,1,0:T(8,128)(2,1)} %bitcast.5, f32[2,320,320]{2,1,0:T(8,128)} %bitcast.6), custom_call_target="tpu_custom_call" | custom-call | flops 4294967296 | bytes 6291456 | tf_op jit(solution)/shard_map/cycle/pallas_call | solution.py:416
  29.1 0.9 %unpack.1 = bf16[1,2,2,23040]{3,2,1,0:T(2,128)(2,1)} custom-call(bf16[144,640]{1,0:T(8,128)(2,1)S(1)} %cycle.1.pair), custom_call_target="tpu_custom_call" | custom-call | tf_op jit(solution)/shard_map/unpack/pallas_call | solution.py:470

commit v6 on v5

--- a/solution.py
+++ b/solution.py
@@ -10,6 +10,7 @@
 C = 320
 W = 72
 STEPS = 2
+CHAIN = 8
 FRAMES = 2
 SEGMENTS = 4
 GROUPS = 64
@@ -150,7 +151,7 @@
     out,
     raw_x, strip, pixels, raw_s, raw_t, raw_b, wm, w_near, w_own, w_far, w_hid, we, e_near, e_own, e_far, e_hid, wt_main, wt_rest, wt_ends,
     packed, arrived, hidden, xm, xr, hm, hr, zf, zh, zfe, zhe,
-    load_sem, send_sem, recv_sem,
+    load_sem, send_sem, recv_sem, go_sem,
 ):
     segment = lax.axis_index("segment")
     group = lax.axis_index("rows")
@@ -159,6 +160,9 @@
     across = group - 1 + 2 * core
     inner = group + 1 - 2 * core
     has_across = (across >= 0) & (across < GROUPS)
+    edge = lax.rem(group, CHAIN)
+    goes_first = has_across & (edge == 0)
+    goes_after = (edge == 1) & (group > 1)
 
     loads = []
     for slot in range(2):
@@ -218,8 +222,22 @@
         return piece(step, 2, part, arrived.at[step, 1], arrived.at[step, 2], (segment, inner))
 
     parts = range(len(PARTS))
-    for part in parts:
-        own_copy(0, part).start()
+
+    def send(step):
+        @pl.when(goes_after)
+        def _():
+            pl.semaphore_wait(go_sem.at[step], 1)
+
+        for part in parts:
+            own_copy(step, part).start()
+
+        @pl.when(goes_first)
+        def _():
+            for part in range(1):
+                own_copy(step, part).wait_send()
+            pl.semaphore_signal(go_sem.at[step], inc=1, device_id=(segment, inner), device_id_type=MESH)
+
+    send(0)
 
     @pl.when(jnp.logical_not(has_across))
     def _():
@@ -371,15 +389,20 @@
         rest = jnp.where(two, rest, centre[2])
         if step + 1 < STEPS:
             packed[step + 1] = jnp.concatenate([main_a, main_b, rest], axis=1).astype(BF16)
-            for part in parts:
-                own_copy(step + 1, part).start()
+            send(step + 1)
         else:
             out[...] = jnp.concatenate([main_a, main_b, rest], axis=1).astype(BF16)
 
     for step in range(STEPS):
         for part in parts:
-            own_copy(step, part).wait_send()
             inner_copy(step, part).wait_send()
+            if part >= 1:
+                own_copy(step, part).wait_send()
+
+        @pl.when(jnp.logical_not(goes_first))
+        def _(step=step):
+            for part in range(1):
+                own_copy(step, part).wait_send()
 
         @pl.when(has_across)
         def _(step=step):
@@ -452,6 +475,7 @@
             pltpu.SemaphoreType.DMA((3, 3)),
             pltpu.SemaphoreType.DMA((STEPS, 3, len(PARTS))),
             pltpu.SemaphoreType.DMA((STEPS, 3, len(PARTS))),
+            pltpu.SemaphoreType.REGULAR((STEPS,)),
         ],
         compiler_params=pltpu.CompilerParams(
             collective_id=1, has_side_effects=True, vmem_limit_bytes=56 << 20

time: 30.1 us -> 29.5 us (0.980)
  Pallas kernels: 30 us -> 29.4 us
    pallas_call x1, Pallas kernels: 29.1 us -> 28.5 us  [body(): pl.pallas_call(kernel, out_shape=pltpu.VMEM((PIX, PACK), BF16), in_specs=...]
where the time goes in v6:
time: 29.5 us; the launch traced here: 29.4 us
  Pallas kernels  29.4 us (100%)
    pallas_call x1, Pallas kernels, body(): pl.pallas_call(kernel, out_shape=pltpu.VMEM((PIX, PACK), BF16), in_specs=...  28.5 us
    pallas_call x1, Pallas kernels, body(): pl.pallas_call(unpack, out_shape=jax.ShapeDtypeStruct((1, FRAMES, 2, W *...  0.92 us

profile of v6, /device:TPU:103, one launch (start us, length us, event | category | flops | bytes accessed | tf_op | source)
XLA Modules:
  0.0 29.4 jit_solution(3214852519289215484)
XLA Ops:
  0.0 28.5 %cycle.1.pair = bf16[144,640]{1,0:T(8,128)(2,1)S(1)} custom-call(bf16[1,2,2,23040]{3,2,1,0:T(2,128)(2,1)} %state.1, s32[5]{0:T(128)} %bounds.1, s32[2]{0:T(128)} %timesteps.1, f32[2,320]{1,0:T(2,128)} %bitcast.7, bf16[2,9,320,320]{3,2,1,0:T(8,128)(2,1)} %bitcast.4, bf16[2,3,320,320]{3,2,1,0:T(8,128)(2,1)} %bitcast.5, f32[2,320,320]{2,1,0:T(8,128)} %bitcast.6), custom_call_target="tpu_custom_call" | custom-call | flops 4294967296 | bytes 6291456 | tf_op jit(solution)/shard_map/cycle/pallas_call | solution.py:439
  28.5 0.9 %unpack.1 = bf16[1,2,2,23040]{3,2,1,0:T(2,128)(2,1)} custom-call(bf16[144,640]{1,0:T(8,128)(2,1)S(1)} %cycle.1.pair), custom_call_target="tpu_custom_call" | custom-call | tf_op jit(solution)/shard_map/unpack/pallas_call | solution.py:494

commit v7 on v6

--- a/solution.py
+++ b/solution.py
@@ -161,8 +161,9 @@
     inner = group + 1 - 2 * core
     has_across = (across >= 0) & (across < GROUPS)
     edge = lax.rem(group, CHAIN)
-    goes_first = has_across & (edge == 0)
-    goes_after = (edge == 1) & (group > 1)
+    leader = jnp.where(edge < 2, 0, 1)
+    goes_first = core == leader
+    goes_after = core != leader
 
     loads = []
     for slot in range(2):

time: 29.5 us -> 29.5 us (level)
  no operation moved by 1% of the time
where the time goes in v7:
time: 29.5 us; the launch traced here: 29.4 us
  Pallas kernels  29.4 us (100%)
    pallas_call x1, Pallas kernels, body(): pl.pallas_call(kernel, out_shape=pltpu.VMEM((PIX, PACK), BF16), in_specs=...  28.5 us
    pallas_call x1, Pallas kernels, body(): pl.pallas_call(unpack, out_shape=jax.ShapeDtypeStruct((1, FRAMES, 2, W *...  0.92 us

profile of v7, /device:TPU:103, one launch (start us, length us, event | category | flops | bytes accessed | tf_op | source)
XLA Modules:
  0.0 29.4 jit_solution(1077560455189289371)
XLA Ops:
  0.0 28.5 %cycle.1.pair = bf16[144,640]{1,0:T(8,128)(2,1)S(1)} custom-call(bf16[1,2,2,23040]{3,2,1,0:T(2,128)(2,1)} %state.1, s32[5]{0:T(128)} %bounds.1, s32[2]{0:T(128)} %timesteps.1, f32[2,320]{1,0:T(2,128)} %bitcast.7, bf16[2,9,320,320]{3,2,1,0:T(8,128)(2,1)} %bitcast.4, bf16[2,3,320,320]{3,2,1,0:T(8,128)(2,1)} %bitcast.5, f32[2,320,320]{2,1,0:T(8,128)} %bitcast.6), custom_call_target="tpu_custom_call" | custom-call | flops 4294967296 | bytes 6291456 | tf_op jit(solution)/shard_map/cycle/pallas_call | solution.py:440
  28.5 0.9 %unpack.1 = bf16[1,2,2,23040]{3,2,1,0:T(2,128)(2,1)} custom-call(bf16[144,640]{1,0:T(8,128)(2,1)S(1)} %cycle.1.pair), custom_call_target="tpu_custom_call" | custom-call | tf_op jit(solution)/shard_map/unpack/pallas_call | solution.py:495
